TPU v7x, 256 devices: a whole 4x4x8 slice. The times are simulated.
256 devices in a mesh: rows: 32 (over y, x, core), cols: 8 (over z).
Axes of the slice: x: 4, y: 4, z: 8, core: 2. Of those that a mesh axis runs over, the one named last changes fastest.
Arguments:
- samples: float32 [2, 16384, 4096], P(None, 'rows', 'cols'), may hold values from -6 to 6
- sketch: float32 [2, 4096, 256], P(None, 'cols'), may hold values from -0.0625 to 0.0625
Outputs:
- basis: float32 [2, 16384, 512], P(None, 'rows')
- projected: float32 [2, 512, 4096], P(None, None, 'cols')
All inputs are finite; a program needn't handle non-finite values.
Results may differ from a plain program's by a relative error of at most 0.000088.
Values sent between devices are 32-bit elements; how exact they have to be, the bound alone decides.
A program may use at most 64 MiB of HBM per device.

v0:
```python
import jax
import jax.numpy as jnp
from jax import lax
from jax.sharding import PartitionSpec as P

HI = lax.Precision.HIGHEST


def mult(left, right):
    return jnp.dot(left, right, precision=HI, preferred_element_type=jnp.float32)


def mult_t(left, right):
    return lax.dot_general(
        left, right, (((0,), (0,)), ((), ())), precision=HI, preferred_element_type=jnp.float32
    )


def forward(real_a, imag_a, pair):
    return jnp.stack(
        [
            mult(real_a, pair[0]) - mult(imag_a, pair[1]),
            mult(real_a, pair[1]) + mult(imag_a, pair[0]),
        ]
    )


def gram_terms(pair):
    gram_r = mult_t(pair[0], pair[0]) + mult_t(pair[1], pair[1])
    gram_i = mult_t(pair[0], pair[1]) - mult_t(pair[1], pair[0])
    return (gram_r, gram_i)


def per_device(samples, sketch):
    real_a, imag_a = (samples[0], samples[1])
    first = lax.psum(forward(real_a, imag_a, sketch), "cols")
    back_part = jnp.stack(
        [
            mult_t(real_a, first[0]) + mult_t(imag_a, first[1]),
            mult_t(real_a, first[1]) - mult_t(imag_a, first[0]),
        ]
    )
    back = lax.psum(back_part, "rows")
    power_part = forward(real_a, imag_a, back)
    power = lax.psum(power_part, "cols")
    gram_r, gram_i = lax.psum(gram_terms(power), "rows")
    gram = jnp.concatenate(
        [jnp.concatenate([gram_r, -gram_i], 1), jnp.concatenate([gram_i, gram_r], 1)], 0
    )
    lower = jnp.linalg.cholesky(gram)
    upper_rows = jnp.concatenate([power[0], -power[1]], 1)
    lower_rows = jnp.concatenate([power[1], power[0]], 1)
    basis_top = lax.linalg.triangular_solve(
        lower, upper_rows, left_side=False, lower=True, transpose_a=True
    )
    basis_bot = lax.linalg.triangular_solve(
        lower, lower_rows, left_side=False, lower=True, transpose_a=True
    )
    proj_part = jnp.stack(
        [
            mult_t(basis_top, real_a) + mult_t(basis_bot, imag_a),
            mult_t(basis_bot, real_a) - mult_t(basis_top, imag_a),
        ]
    )
    projected = lax.psum(proj_part, "rows")
    total_rows = samples.shape[1] * lax.axis_size("rows")
    scale = jnp.sqrt(jnp.float32(2 * total_rows))
    basis = jnp.stack([basis_top, basis_bot]) * scale
    return (basis, projected)


def solution(mesh):
    placed = (P(None, "rows", "cols"), P(None, "cols", None))
    return jax.shard_map(
        per_device,
        mesh=mesh,
        in_specs=placed,
        out_specs=(P(None, "rows", None), P(None, None, "cols")),
        check_vma=False,
    )
```

profile of v0, /device:TPU:1, one launch (start us, length us, event | category | flops | bytes accessed | tf_op | source)
XLA Modules:
  0.0 712.4 jit_solution(4775538029646054761)
XLA Ops:
  7.2 2.5 fusion.29
  9.7 2.0 fusion.31
  14.9 75.7 %all-reduce.8.cloned.1.call-done = f32[2,512,256]{2,1,0:T(8,128)} async-done(((f32[2,512,256]{2,1,0:T(8,128)}), f32[2,512,256]{2,1,0:T(8,128)}) %all-reduce.8.cloned.1.call-update) | async-done | bytes 1048592 | tf_op jit(solution)/shard_map/psum | solution.py:36
  90.6 2.2 fusion.25
  97.3 117.4 %all-reduce.10.cloned.1.call-done = f32[2,512,256]{1,2,0:T(8,128)} async-done(((f32[2,512,256]{1,2,0:T(8,128)}), f32[2,512,256]{1,2,0:T(8,128)}) %all-reduce.10.cloned.1.call-update) | async-done | bytes 1048592 | tf_op jit(solution)/shard_map/psum | solution.py:43
  214.7 2.2 fusion.21
  221.2 71.7 %all-reduce.12.cloned.1.call-done = f32[2,512,256]{1,2,0:T(8,128)} async-done(((f32[2,512,256]{1,2,0:T(8,128)}), f32[2,512,256]{1,2,0:T(8,128)}) %all-reduce.12.cloned.1.call-update) | async-done | bytes 1048592 | tf_op jit(solution)/shard_map/psum | solution.py:45
  293.0 1.9 fusion.111
  294.9 1.8 fusion.110
  301.7 114.0 %all-reduce.16.cloned.1.call-done = (f32[256,256]{0,1:T(8,128)}, f32[256,256]{0,1:T(8,128)}) async-done(((f32[256,256]{0,1:T(8,128)}, f32[256,256]{0,1:T(8,128)}), (f32[256,256]{0,1:T(8,128)}, f32[256,256]{0,1:T(8,128)})) %all-reduce.16.cloned.1.call-update) | async-done | bytes 524304 | tf_op jit(solution)/shard_map/psum | solution.py:46
  419.9 1.6 fusion.8
  422.5 11.7 %cholesky.104 = f32[128,128]{1,0:T(8,128)S(1)} custom-call(f32[128,128]{1,0:T(8,128)S(1)} %cholesky.266), custom_call_target="Cholesky" | custom-call | tf_op jit(solution)/shard_map/jit(cholesky)/cholesky | solution.py:50
  434.3 9.8 %custom-call.30 = f32[1,128,128]{1,2,0:T(8,128)S(1)} custom-call(f32[1,128,128]{2,1,0:T(8,128)S(1)} %get-tuple-element.44), custom_call_target="InvertDiagBlocksLowerTriangular" | custom-call | tf_op jit(solution)/shard_map/jit(cholesky)/cholesky | solution.py:50
  446.8 11.7 %cholesky.217 = f32[128,128]{1,0:T(8,128)S(1)} custom-call(f32[128,128]{1,0:T(8,128)S(1)} %cholesky.270), custom_call_target="Cholesky" | custom-call | tf_op jit(solution)/shard_map/jit(cholesky)/cholesky | solution.py:50
  458.5 9.9 %custom-call.31 = f32[1,128,128]{1,2,0:T(8,128)S(1)} custom-call(f32[1,128,128]{2,1,0:T(8,128)S(1)} %get-tuple-element.41), custom_call_target="InvertDiagBlocksLowerTriangular" | custom-call | tf_op jit(solution)/shard_map/jit(cholesky)/cholesky | solution.py:50
  470.0 11.7 %cholesky.238 = f32[128,128]{1,0:T(8,128)S(1)} custom-call(f32[128,128]{1,0:T(8,128)S(1)} %cholesky.275), custom_call_target="Cholesky" | custom-call | tf_op jit(solution)/shard_map/jit(cholesky)/cholesky | solution.py:50
  482.4 9.8 %custom-call.32 = f32[1,128,128]{1,2,0:T(8,128)S(1)} custom-call(f32[1,128,128]{2,1,0:T(8,128)S(1)} %get-tuple-element.38), custom_call_target="InvertDiagBlocksLowerTriangular" | custom-call | tf_op jit(solution)/shard_map/jit(cholesky)/cholesky | solution.py:50
  493.7 11.7 %cholesky.255 = f32[128,128]{1,0:T(8,128)S(1)} custom-call(f32[128,128]{1,0:T(8,128)S(1)} %convolution_subtract_fusion.13), custom_call_target="Cholesky" | custom-call | tf_op jit(solution)/shard_map/jit(cholesky)/cholesky | solution.py:50
  510.4 14.1 %while.4 = (s32[]{:T(128)}, f32[512,512]{1,0:T(8,128)}, s32[4,2]{0,1:T(2,128)S(1)}, f32[4,128,128]{2,1,0:T(8,128)}, s32[]{:T(128)}) while((s32[]{:T(128)}, f32[512,512]{1,0:T(8,128)}, s32[4,2]{0,1:T(2,128)S(1)}, f32[4,128,128]{2,1,0:T(8,128)}, s32[]{:T(128)}) %tuple.38), condition=%wide.while_cond, body=%wide.while_body.sunk | while | flops 2 | bytes 132205 | solution.py:53
  511.1 2.9 bitcast_dynamic-update-slice_fusion.2
  514.6 2.9 bitcast_dynamic-update-slice_fusion.2
  518.2 2.9 bitcast_dynamic-update-slice_fusion.2
  521.7 2.8 bitcast_dynamic-update-slice_fusion.2
  524.5 40.3 %custom-call.34 = f32[4,128,128]{1,2,0:T(8,128)S(1)} custom-call(f32[4,128,128]{2,1,0:T(8,128)} %get-tuple-element.17), custom_call_target="InvertDiagBlocksLowerTriangular" | custom-call | tf_op jit(solution)/shard_map/triangular_solve/custom-call.3 | solution.py:53
  576.2 1.9 fusion.17
  578.1 1.9 fusion.19
  580.0 1.9 fusion
  581.8 1.9 fusion.1
  583.7 1.5 pad_maximum_fusion
  586.7 1.8 copy.9
  588.5 114.0 %all-reduce.14.cloned.1.call-done = f32[2,512,512]{2,1,0:T(8,128)} async-done(((f32[2,512,512]{2,1,0:T(8,128)}), f32[2,512,512]{2,1,0:T(8,128)}) %all-reduce.14.cloned.1.call-update) | async-done | bytes 2097168 | tf_op jit(solution)/shard_map/psum | solution.py:65
  702.4 3.1 copy.35
  (114 shorter events, 46.0 us)
Async XLA Ops:
  7.2 2.6 copy-start
  7.2 4.6 copy-start.7
  7.2 83.4 %all-reduce.8.cloned.1.call-start = ((), (), s32[]{:S(2)}) async-start(), calls=%async_computation | async-start | bytes 2097152 | tf_op jit(solution)/shard_map/psum | solution.py:36
  14.8 199.9 %all-reduce.10.cloned.1.call-start = ((), (), s32[]{:S(2)}) async-start(), calls=%async_computation.1 | async-start | bytes 2097152 | tf_op jit(solution)/shard_map/psum | solution.py:43
  90.6 2.2 copy-start.8
  97.1 195.9 %all-reduce.12.cloned.1.call-start = ((), (), s32[]{:S(2)}) async-start(), calls=%async_computation.2 | async-start | bytes 2097152 | tf_op jit(solution)/shard_map/psum | solution.py:45
  214.7 2.2 copy-start.9
  221.2 194.6 %all-reduce.16.cloned.1.call-start = ((), (), s32[]{:S(2)}) async-start(), calls=%async_computation.4 | async-start | bytes 1048576 | tf_op jit(solution)/shard_map/psum | solution.py:46
  293.0 3.7 copy-start.1
  299.4 403.1 %all-reduce.14.cloned.1.call-start = ((), (), s32[]{:S(2)}) async-start(), calls=%async_computation.3 | async-start | bytes 4194304 | tf_op jit(solution)/shard_map/psum | solution.py:65
  416.7 0.7 copy-start.16
  416.7 3.2 copy-start.15
  421.6 1.0 copy-start.14
  510.4 57.8 %copy-start.4 = (f32[512,256]{0,1:T(8,128)S(1)}, f32[512,256]{0,1:T(8,128)}, u32[]{:S(2)}) copy-start(f32[512,256]{0,1:T(8,128)} %get-tuple-element.33) | copy-start | bytes 1572868
  564.9 3.3 copy-start.18
  564.9 4.7 copy-start.6
  567.8 5.4 copy-start.17
  568.2 4.5 copy-start.19
  570.0 4.3 copy-start.5
  574.2 5.7 copy-start.10
  575.1 6.7 copy-start.2
  576.2 5.6 copy-start.12
  585.2 0.9 copy-start.3
  585.2 1.0 copy-start.13
  585.2 1.1 copy-start.11
Sparse Core Ops, SparseCore 0:
  15.0 75.5 all-reduce.7
  97.2 117.4 all-reduce.9
  221.3 71.6 all-reduce.11
  299.5 116.2 all-reduce.15
  585.3 117.0 all-reduce.13
where the time goes:
time: 720 us; the launch traced here: 712 us
  waiting for transfers between devices  493 us (68%)
  other arithmetic  130 us (18%)
  matrix products  47.6 us (7%)
  local copies, waits for them, and re-layouts  24.2 us (3%)
  between operations  17.3 us (2%)
    psum x1, waiting for transfers between devices, per_device(): back = lax.psum(back_part, 'rows')  117 us
    psum x1, waiting for transfers between devices, per_device(): gram_r, gram_i = lax.psum(gram_terms(power), 'rows')  114 us
    psum x1, waiting for transfers between devices, per_device(): projected = lax.psum(proj_part, 'rows')  114 us
    another operation x14, other arithmetic, per_device(): lower = jnp.linalg.cholesky(gram)  78.6 us
    psum x1, waiting for transfers between devices, per_device(): first = lax.psum(forward(real_a, imag_a, sketch), 'cols')  75.7 us
    psum x1, waiting for transfers between devices, per_device(): power = lax.psum(power_part, 'cols')  71.7 us
    another operation x4, other arithmetic, per_device(): lax.linalg.triangular_solve(lower, upper_rows, left_side=False, lower=Tru...  41.4 us
    dot_general x12, matrix products, mult_t(): lax.dot_general(left, right, (((0,), (0,)), ((), ())), precision=HI, pref...  19.2 us
  transfers between devices with their start and end apart: 5, of which 5 were waited for; matrix products, arithmetic and copies ran while one was open for 1% of the time, Pallas kernels for 0%

commit v1 on v0

v1 whole, which is shorter than its diff:
```python
import functools

import jax
import jax.numpy as jnp
from jax import lax
from jax.experimental import pallas as pl
from jax.experimental.pallas import tpu as pltpu
from jax.sharding import PartitionSpec as P

MESH = pl.DeviceIdType.MESH
HI = lax.Precision.HIGHEST
F32 = jnp.float32
BF16 = jnp.bfloat16

Z_SLOTS = 28
ROW_SLOTS = 34
GRAM_SLOTS = 21


def split(value):
    high = value.astype(BF16)
    return high, (value - high.astype(F32)).astype(BF16)


class Copies:
    def __init__(self, send_sem, recv_sem):
        self.send_sem, self.recv_sem = send_sem, recv_sem
        self.made = {}

    def send(self, slot, src, dst, device):
        copy = pltpu.make_async_remote_copy(
            src_ref=src, dst_ref=dst, send_sem=self.send_sem.at[slot],
            recv_sem=self.recv_sem.at[slot], device_id=device, device_id_type=MESH,
        )
        copy.start()
        self.made[slot] = copy

    def arrived(self, slot):
        self.made[slot].wait_recv()

    def finish(self):
        for copy in self.made.values():
            copy.wait_send()


class Place:
    def __init__(self):
        self.r = lax.axis_index("rows")
        self.z = lax.axis_index("cols")
        self.core = lax.rem(self.r, 2)
        self.x = lax.rem(self.r // 2, 4)
        self.y = self.r // 8

    def along_z(self, d):
        return (self.r, lax.rem(self.z + d + 8, 8))

    def along_x(self, d):
        return ((self.y * 4 + lax.rem(self.x + d, 4)) * 2 + self.core, self.z)

    def along_y(self, d):
        return ((lax.rem(self.y + d, 4) * 4 + self.x) * 2 + self.core, self.z)

    def sibling(self):
        return (self.r + 1 - 2 * self.core, self.z)

    def line(self, axis, d):
        return self.along_x(d) if axis == 0 else self.along_y(d)

    def at(self, axis):
        return self.x if axis == 0 else self.y


def greet(place):
    barrier = pltpu.get_barrier_semaphore()
    peers = [place.sibling()]
    peers += [place.along_x(d) for d in (1, 2, 3)]
    peers += [place.along_y(d) for d in (1, 2, 3)]
    peers += [place.along_z(d) for d in range(1, 8)]
    for peer in peers:
        pl.semaphore_signal(barrier, inc=1, device_id=peer, device_id_type=MESH)
    pl.semaphore_wait(barrier, len(peers))


def wrap8(value):
    return lax.rem(value + 16, 8)


class RingZ:
    def __init__(self, place, copies, base, part, slots, full):
        self.place, self.copies, self.base = place, copies, base
        self.part, self.slots, self.full = part, slots, full

    def scatter_steps(self):
        place, copies, part, slots = self.place, self.copies, self.part, self.slots

        def slot(way, half, dist):
            return self.base + (0 if way > 0 else 7) + (dist - 1 if half == lead(way) else 3 + dist)

        def lead(way):
            return 0 if way > 0 else 1

        def box(way, half, dist):
            return (0 if way > 0 else 7) + (dist - 1 if half == lead(way) else 3 + dist)

        def push(way, half, dist):
            chunk = wrap8(place.z + way * dist)
            copies.send(slot(way, half, dist), part.at[chunk, half], slots.at[box(way, half, dist)],
                        place.along_z(way))

        def pull(way, half, dist):
            copies.arrived(slot(way, half, dist))
            chunk = wrap8(place.z + way * (dist - 1))
            part[chunk, half] = part[chunk, half] + slots[box(way, half, dist)]

        for way in (1, -1):
            push(way, lead(way), 4)
        for way in (1, -1):
            push(way, 1 - lead(way), 3)
        yield
        for step in range(3):
            for way in (1, -1):
                half = lead(way)
                pull(way, half, 4 - step)
                push(way, half, 3 - step)
            for way in (1, -1):
                half = 1 - lead(way)
                pull(way, half, 3 - step)
                if step < 2:
                    push(way, half, 2 - step)
            yield
        for way in (1, -1):
            pull(way, lead(way), 1)
        yield

    def gather_steps(self):
        place, copies, full, part = self.place, self.copies, self.full, self.part
        me = place.z
        full[me] = part[me]
        base = self.base + 14

        def slot(way, half, dist):
            return base + (0 if way > 0 else 7) + (dist * 2 + half if dist < 3 else 6)

        def push(way, half, dist):
            chunk = wrap8(me - way * dist)
            ref = full.at[chunk, half]
            copies.send(slot(way, half, dist), ref, ref, place.along_z(way))

        for half in (0, 1):
            for way in (1, -1):
                push(way, half, 0)
        yield
        for dist in (1, 2):
            for half in (0, 1):
                for way in (1, -1):
                    copies.arrived(slot(way, half, dist - 1))
                    push(way, half, dist)
            yield
        for half in (0, 1):
            for way in (1, -1):
                copies.arrived(slot(way, half, 2))
                if half == (0 if way > 0 else 1):
                    push(way, half, 3)
        yield
        for way in (1, -1):
            copies.arrived(slot(way, 0 if way > 0 else 1, 3))
        yield


class SumRows:
    def __init__(self, place, copies, base, part, from_core, from_line, from_point, full):
        self.place, self.copies, self.base = place, copies, base
        self.part, self.full = part, full
        self.from_core, self.from_line, self.from_point = from_core, from_line, from_point

    def steps(self):
        place, copies, base = self.place, self.copies, self.base
        part, full, core = self.part, self.full, place.core
        first = [place.at(0), place.at(1)]
        second = [place.at(1), place.at(0)]
        for h in (0, 1):
            copies.send(base + h, part.at[h, 1 - core], self.from_core.at[h], place.sibling())
        yield
        base += 2
        for h in (0, 1):
            copies.arrived(base - 2 + h)
            for d in (2, 1, 3):
                at = lax.rem(first[h] + d, 4)
                part[h, core, at] = part[h, core, at] + self.from_core[h, at]
                copies.send(base + 3 * h + d - 1, part.at[h, core, at], self.from_line.at[h, d - 1],
                            place.line(h, d))
            at = first[h]
            part[h, core, at] = part[h, core, at] + self.from_core[h, at]
        yield
        base += 6
        for h in (0, 1):
            a = first[h]
            for d in (1, 2, 3):
                copies.arrived(base - 6 + 3 * h + d - 1)
            part[h, core, a] = (part[h, core, a] + self.from_line[h, 0]) + (
                self.from_line[h, 1] + self.from_line[h, 2])
            for d in (2, 1, 3):
                b = lax.rem(second[h] + d, 4)
                copies.send(base + 3 * h + d - 1, part.at[h, core, a, b], self.from_point.at[h, d - 1],
                            place.line(1 - h, d))
        yield
        base += 6
        for h in (0, 1):
            a, b = first[h], second[h]
            for d in (1, 2, 3):
                copies.arrived(base - 6 + 3 * h + d - 1)
            full[h, core, a, b] = (part[h, core, a, b] + self.from_point[h, 0]) + (
                self.from_point[h, 1] + self.from_point[h, 2])
            for d in (2, 1, 3):
                ref = full.at[h, core, a, b]
                copies.send(base + 3 * h + d - 1, ref, ref, place.line(1 - h, d))
        yield
        base += 6
        for h in (0, 1):
            a = first[h]
            for d in (1, 2, 3):
                copies.arrived(base - 6 + 3 * h + d - 1)
            ref = full.at[h, core, a]
            for d in (2, 1, 3):
                copies.send(base + 3 * h + d - 1, ref, ref, place.line(h, d))
            copies.send(base + 6 + 4 * h, ref, ref, place.sibling())
        yield
        for h in (0, 1):
            for d in (1, 3, 2):
                copies.arrived(base + 3 * h + d - 1)
                ref = full.at[h, core, lax.rem(first[h] - d + 4, 4)]
                copies.send(base + 6 + 4 * h + d, ref, ref, place.sibling())
        yield
        for h in (0, 1):
            for d in range(4):
                copies.arrived(base + 6 + 4 * h + d)
        yield


class SumAll:
    def __init__(self, place, copies, base, part, from_core, from_line, from_point, from_z, full):
        self.place, self.copies, self.base = place, copies, base
        self.part, self.full = part, full
        self.from_core, self.from_line, self.from_point, self.from_z = (
            from_core, from_line, from_point, from_z)

    def steps(self):
        place, copies, base = self.place, self.copies, self.base
        part, full, core, x, y = self.part, self.full, place.core, place.x, place.y
        copies.send(base, part.at[1 - core], self.from_core, place.sibling())
        yield
        copies.arrived(base)
        base += 1
        part[core] = part[core] + self.from_core[...]
        for d in (2, 1, 3):
            copies.send(base + d - 1, part.at[core, lax.rem(x + d, 4)], self.from_line.at[d - 1],
                        place.along_x(d))
        yield
        for d in (1, 2, 3):
            copies.arrived(base + d - 1)
        base += 3
        part[core, x] = (part[core, x] + self.from_line[0]) + (self.from_line[1] + self.from_line[2])
        for d in (2, 1, 3):
            copies.send(base + d - 1, part.at[core, x, lax.rem(y + d, 4)], self.from_point.at[d - 1],
                        place.along_y(d))
        yield
        for d in (1, 2, 3):
            copies.arrived(base + d - 1)
        base += 3
        mine = self.from_z.at[place.z]
        mine[...] = (part[core, x, y] + self.from_point[0]) + (self.from_point[1] + self.from_point[2])
        for d in (4, 3, 5, 2, 6, 1, 7):
            copies.send(base + d - 1, mine, mine, place.along_z(d))
        yield
        for d in range(1, 8):
            copies.arrived(base + d - 1)
        base += 7
        total = self.from_z[0]
        for z in range(1, 8):
            total = total + self.from_z[z]
        full[core, x, y] = total
        ref = full.at[core, x, y]
        for d in (2, 1, 3):
            copies.send(base + d - 1, ref, ref, place.along_y(d))
        yield
        for d in (1, 2, 3):
            copies.arrived(base + d - 1)
        base += 3
        ref = full.at[core, x]
        for d in (2, 1, 3):
            copies.send(base + d - 1, ref, ref, place.along_x(d))
        yield
        for d in (1, 2, 3):
            copies.arrived(base + d - 1)
        base += 3
        ref = full.at[core]
        copies.send(base, ref, ref, place.sibling())
        yield
        copies.arrived(base)
        yield


def run(steps):
    for _ in steps:
        pass


def interleave(*many):
    live = list(many)
    while live:
        live = [one for one in live if next(one, run) is None]


def multiply(x_hi, x_lo, t_hi, t_lo, store):
    def tile(i, j):
        rows, lanes = pl.ds(i * 256, 256), pl.ds(j * 256, 256)
        xh, xl = x_hi[rows, :], x_lo[rows, :]
        th, tl = t_hi[:, lanes], t_lo[:, lanes]
        dot = functools.partial(jnp.dot, preferred_element_type=F32)
        store(i, j, dot(xh, th) + (dot(xh, tl) + dot(xl, th)))

    @pl.loop(0, 2)
    def _(i):
        for j in range(2):
            tile(i, j)


def power_kernel(a_ref, s_ref, y_ref, b_ref, g_ref, x_hi, x_lo, xt_hi, xt_lo, t_hi, t_lo,
                 z_part, z_slots, z_full, z_part2, z_slots2,
                 r_part, r_core, r_line, r_point, r_full, r_part2, r_core2, r_line2, r_point2,
                 g_part, g_core, g_line, g_point, g_z, send_sem, recv_sem):
    place = Place()
    greet(place)
    copies = Copies(send_sem, recv_sem)

    def set_pair(rows, real, imag, sign):
        low = pl.ds(rows, real.shape[0])
        high = pl.ds(512 + rows, real.shape[0])
        for at, lanes, value in (
            (low, slice(0, 256), real), (low, slice(256, 512), imag),
            (high, slice(0, 256), sign * imag), (high, slice(256, 512), -sign * real),
        ):
            t_hi[at, lanes], t_lo[at, lanes] = split(value)

    @pl.loop(0, 8)
    def _(i):
        rows = pl.ds(i * 64, 64)
        for p in (0, 1):
            x_hi[rows, p * 512:(p + 1) * 512], x_lo[rows, p * 512:(p + 1) * 512] = split(a_ref[p, rows, :])
        set_pair(i * 64, s_ref[0, rows, :], s_ref[1, rows, :], -1.0)

    def store_chunks(ref):
        def store(i, j, tile):
            ref[pl.ds(i * 4, 4), :, :, j * 256:(j + 1) * 256] = tile.reshape(4, 2, 32, 256)
        return store

    def store_rows(ref):
        def store(i, j, tile):
            ref[j, i] = tile.reshape(4, 4, 16, 256)
        return store

    multiply(x_hi, x_lo, t_hi, t_lo, store_chunks(z_part))
    ring = RingZ(place, copies, 0, z_part, z_slots, z_full)
    steps = ring.scatter_steps()
    next(steps)

    @pl.loop(0, 4)
    def _(i):
        for p in (0, 1):
            rows = pl.ds(i * 128, 128)
            block = a_ref[p, :, rows].T
            lanes = slice(p * 512, (p + 1) * 512)
            xt_hi[rows, lanes], xt_lo[rows, lanes] = split(block)

    run(steps)
    run(ring.gather_steps())

    def chunks_to_t(ref):
        @pl.loop(0, 8)
        def _(i):
            value = ref[i].reshape(64, 512)
            set_pair(i * 64, value[:, :256], value[:, 256:], 1.0)

    chunks_to_t(z_full)
    multiply(xt_hi, xt_lo, t_hi, t_lo, store_rows(r_part))
    run(SumRows(place, copies, Z_SLOTS, r_part, r_core, r_line, r_point, r_full).steps())

    for k in (0, 1):
        @pl.loop(0, 4)
        def _(i):
            set_pair(k * 256 + i * 64, r_full[0, k, i].reshape(64, 256), r_full[1, k, i].reshape(64, 256), -1.0)

    multiply(x_hi, x_lo, t_hi, t_lo, store_chunks(z_part2))
    ring = RingZ(place, copies, Z_SLOTS + ROW_SLOTS, z_part2, z_slots2, y_ref)
    run(ring.scatter_steps())
    mine = z_part2[place.z].reshape(64, 512)
    steps = ring.gather_steps()
    next(steps)
    real, imag = mine[:, :256], mine[:, 256:]
    tall = jnp.concatenate([real, imag], 0).T
    gram_r = jnp.dot(tall, jnp.concatenate([real, imag], 0), precision=HI, preferred_element_type=F32)
    gram_i = jnp.dot(tall, jnp.concatenate([imag, -real], 0), precision=HI, preferred_element_type=F32)
    low = lax.broadcasted_iota(jnp.int32, (256, 256), 0) >= lax.broadcasted_iota(jnp.int32, (256, 256), 1)
    g_part[...] = jnp.where(low, gram_r, gram_i).reshape(2, 4, 4, 8, 256)
    gram_steps = SumAll(place, copies, 2 * Z_SLOTS + ROW_SLOTS, g_part, g_core, g_line, g_point, g_z, g_ref).steps()
    interleave(gram_steps, steps)

    chunks_to_t(y_ref)
    multiply(xt_hi, xt_lo, t_hi, t_lo, store_rows(r_part2))
    run(SumRows(place, copies, 2 * Z_SLOTS + ROW_SLOTS + GRAM_SLOTS, r_part2, r_core2, r_line2, r_point2,
                b_ref).steps())
    copies.finish()


def power(samples, sketch):
    vmem = pl.BlockSpec(memory_space=pltpu.VMEM)
    slots = 2 * Z_SLOTS + 2 * ROW_SLOTS + GRAM_SLOTS
    chunks = pltpu.VMEM((8, 2, 32, 512), F32)
    boxes = pltpu.VMEM((14, 32, 512), F32)
    rows = [
        pltpu.VMEM((2, 2, 4, 4, 16, 256), F32),
        pltpu.VMEM((2, 4, 4, 16, 256), F32),
        pltpu.VMEM((2, 3, 4, 16, 256), F32),
        pltpu.VMEM((2, 3, 16, 256), F32),
    ]
    return pl.pallas_call(
        power_kernel,
        out_shape=(
            jax.ShapeDtypeStruct((8, 2, 32, 512), F32),
            jax.ShapeDtypeStruct((2, 2, 4, 4, 16, 256), F32),
            jax.ShapeDtypeStruct((2, 4, 4, 8, 256), F32),
        ),
        in_specs=[vmem] * 2,
        out_specs=(vmem,) * 3,
        scratch_shapes=[
            *[pltpu.VMEM((512, 1024), BF16)] * 4,
            *[pltpu.VMEM((1024, 512), BF16)] * 2,
            chunks, boxes, chunks, chunks, boxes,
            *rows, pltpu.VMEM((2, 2, 4, 4, 16, 256), F32), *rows,
            pltpu.VMEM((2, 4, 4, 8, 256), F32),
            pltpu.VMEM((4, 4, 8, 256), F32),
            pltpu.VMEM((3, 4, 8, 256), F32),
            pltpu.VMEM((3, 8, 256), F32),
            pltpu.VMEM((8, 8, 256), F32),
            pltpu.SemaphoreType.DMA((slots,)),
            pltpu.SemaphoreType.DMA((slots,)),
        ],
        compiler_params=pltpu.CompilerParams(
            collective_id=0, has_side_effects=True, vmem_limit_bytes=48 * 2**20
        ),
        name="power",
    )(samples, sketch)


def mult(left, right):
    return jnp.dot(left, right, precision=HI, preferred_element_type=F32)


def per_device(samples, sketch):
    y, b, packed = power(samples, sketch)
    y = y.reshape(512, 512)
    b = b.reshape(2, 512, 256)
    packed = packed.reshape(256, 256)
    gram_r = jnp.tril(packed) + jnp.tril(packed, -1).T
    gram_i = jnp.triu(packed, 1) - jnp.triu(packed, 1).T
    gram = jnp.concatenate(
        [jnp.concatenate([gram_r, -gram_i], 1), jnp.concatenate([gram_i, gram_r], 1)], 0
    )
    lower = jnp.linalg.cholesky(gram)
    inverse = lax.linalg.triangular_solve(lower, jnp.eye(512, dtype=F32), left_side=True, lower=True)
    yr, yi = y[:, :256], y[:, 256:]
    total_rows = samples.shape[1] * lax.axis_size("rows")
    scale = jnp.sqrt(jnp.float32(2 * total_rows))
    top = mult(jnp.concatenate([yr, -yi], 1), inverse.T)
    bot = mult(jnp.concatenate([yi, yr], 1), inverse.T)
    basis = jnp.stack([top, bot]) * scale
    projected = jnp.stack([
        mult(inverse, jnp.concatenate([b[0], -b[1]], 1).T),
        mult(inverse, jnp.concatenate([b[1], b[0]], 1).T),
    ])
    return (basis, projected)


def solution(mesh):
    placed = (P(None, "rows", "cols"), P(None, "cols", None))
    return jax.shard_map(
        per_device,
        mesh=mesh,
        in_specs=placed,
        out_specs=(P(None, "rows", None), P(None, None, "cols")),
        check_vma=False,
    )
```

time: 720 us -> 305 us (0.42)
  waiting for transfers between devices: 493 us -> 0 us
  Pallas kernels: 0 us -> 135 us
  matrix products: 47.6 us -> 18.6 us
  between operations: 17.3 us -> 3.81 us
    psum x5 -> x0, waiting for transfers between devices: 493 us -> none  [the longest x1 117 us: per_device(): back = lax.psum(back_part, 'rows')]
    pallas_call x0 -> x1, Pallas kernels: none -> 135 us  [power(): pl.pallas_call(power_kernel, out_shape=(jax.ShapeDtypeStruct((8, 2, 32, 5...]
    dot_general x20 -> x4, matrix products: 31 us -> 7.47 us  [mult(): return jnp.dot(left, right, precision=HI, preferred_element_type=F32)]
    another operation x10 -> x4, other arithmetic: 46.2 us -> 42 us  [the longest x3 40.4 us: per_device(): lax.linalg.triangular_solve(lower, jnp.eye(512, dtype=F32), left_side=Tru...]
  transfers between devices with their start and end apart: 5 -> 0, of which waited for: 5 -> 0; matrix products, arithmetic and copies ran while one was open for 1% -> 0% of each run, Pallas kernels for 0% -> 0%
where the time goes in v1:
time: 305 us; the launch traced here: 301 us
  Pallas kernels  135 us (44%)
  other arithmetic  126 us (41%)
  matrix products  18.6 us (6%)
  local copies, waits for them, and re-layouts  17.9 us (6%)
  between operations  3.81 us (1%)
    pallas_call x1, Pallas kernels, power(): pl.pallas_call(power_kernel, out_shape=(jax.ShapeDtypeStruct((8, 2, 32, 5...  135 us
    another operation x14, other arithmetic, per_device(): lower = jnp.linalg.cholesky(gram)  78.8 us
    another operation x3, other arithmetic, per_device(): lax.linalg.triangular_solve(lower, jnp.eye(512, dtype=F32), left_side=Tru...  40.4 us
    another operation x12, local copies, waits for them, and re-layouts  11.6 us
    dot_general x4, matrix products, mult(): return jnp.dot(left, right, precision=HI, preferred_element_type=F32)  7.47 us

profile of v1, /device:TPU:1, one launch (start us, length us, event | category | flops | bytes accessed | tf_op | source)
XLA Modules:
  0.0 301.0 jit_solution(7676931330390407500)
XLA Ops:
  0.6 1.6 copy-done
  2.2 1.2 copy-done.1
  3.4 134.5 %power.1 = (f32[8,2,32,512]{3,2,1,0:T(8,128)S(1)}, f32[2,2,4,4,16,256]{5,4,3,2,1,0:T(8,128)S(1)}, f32[2,4,4,8,256]{4,3,2,1,0:T(8,128)S(1)}) custom-call(f32[2,512,512]{2,1,0:T(8,128)S(1)} %copy-done, f32[2,512,256]{2,1,0:T(8,128)S(1)} %copy-done.1), custom_call_target="tpu_custom_call" | custom-call | tf_op jit(solution)/shard_map/power/pallas_call | solution.py:426
  140.8 1.3 copy.6
  142.1 1.6 fusion.12
  144.7 11.7 %cholesky.104 = f32[128,128]{1,0:T(8,128)S(1)} custom-call(f32[128,128]{1,0:T(8,128)S(1)} %cholesky.266), custom_call_target="Cholesky" | custom-call | tf_op jit(solution)/shard_map/jit(cholesky)/cholesky | solution.py:469
  156.4 9.8 %custom-call.30 = f32[1,128,128]{1,2,0:T(8,128)S(1)} custom-call(f32[1,128,128]{2,1,0:T(8,128)S(1)} %get-tuple-element.45), custom_call_target="InvertDiagBlocksLowerTriangular" | custom-call | tf_op jit(solution)/shard_map/jit(cholesky)/cholesky | solution.py:469
  166.4 1.2 constant_dynamic-update-slice_fusion.3
  167.6 1.3 convolution_subtract_fusion.3
  168.9 11.8 %cholesky.217 = f32[128,128]{1,0:T(8,128)S(1)} custom-call(f32[128,128]{1,0:T(8,128)S(1)} %cholesky.270), custom_call_target="Cholesky" | custom-call | tf_op jit(solution)/shard_map/jit(cholesky)/cholesky | solution.py:469
  182.9 9.8 %custom-call.31 = f32[1,128,128]{1,2,0:T(8,128)S(1)} custom-call(f32[1,128,128]{2,1,0:T(8,128)S(1)} %get-tuple-element.42), custom_call_target="InvertDiagBlocksLowerTriangular" | custom-call | tf_op jit(solution)/shard_map/jit(cholesky)/cholesky | solution.py:469
  193.0 1.3 convolution_subtract_fusion.4
  194.3 11.7 %cholesky.238 = f32[128,128]{1,0:T(8,128)S(1)} custom-call(f32[128,128]{1,0:T(8,128)S(1)} %cholesky.275), custom_call_target="Cholesky" | custom-call | tf_op jit(solution)/shard_map/jit(cholesky)/cholesky | solution.py:469
  207.3 9.8 %custom-call.32 = f32[1,128,128]{1,2,0:T(8,128)S(1)} custom-call(f32[1,128,128]{2,1,0:T(8,128)S(1)} %get-tuple-element.39), custom_call_target="InvertDiagBlocksLowerTriangular" | custom-call | tf_op jit(solution)/shard_map/jit(cholesky)/cholesky | solution.py:469
  217.3 1.2 convolution_subtract_fusion.5
  218.6 11.9 %cholesky.255 = f32[128,128]{1,0:T(8,128)S(1)} custom-call(f32[128,128]{1,0:T(8,128)S(1)} %convolution_subtract_fusion.5), custom_call_target="Cholesky" | custom-call | tf_op jit(solution)/shard_map/jit(cholesky)/cholesky | solution.py:469
  231.8 1.1 select_select_fusion
  232.9 11.7 %while.1 = (s32[]{:T(128)}, f32[512,512]{1,0:T(8,128)}, s32[4,2]{0,1:T(2,128)S(1)}, f32[4,128,128]{2,1,0:T(8,128)S(1)}, s32[]{:T(128)}) while((s32[]{:T(128)}, f32[512,512]{1,0:T(8,128)}, s32[4,2]{0,1:T(2,128)S(1)}, f32[4,128,128]{2,1,0:T(8,128)S(1)}, s32[]{:T(128)}) %tuple.37), condition=%wide.while_cond, body=%wide.while_body.sunk | while | flops 2 | bytes 131181 | solution.py:470
  233.6 2.2 bitcast_dynamic-update-slice_fusion.2
  236.5 2.2 bitcast_dynamic-update-slice_fusion.2
  239.5 2.2 bitcast_dynamic-update-slice_fusion.2
  242.4 2.2 bitcast_dynamic-update-slice_fusion.2
  244.6 39.3 %custom-call.33 = f32[4,128,128]{1,2,0:T(8,128)S(1)} custom-call(f32[4,128,128]{2,1,0:T(8,128)S(1)} %get-tuple-element.15), custom_call_target="InvertDiagBlocksLowerTriangular" | custom-call | tf_op jit(solution)/shard_map/triangular_solve | solution.py:470
  284.5 1.2 convolution_subtract_fusion.1
  286.1 1.3 convolution_subtract_fusion
  287.9 1.6 convolution_subtract_fusion.2
  290.0 1.9 convolution_bitcast_fusion.1
  291.9 1.9 convolution_bitcast_fusion
  293.7 1.5 pad_maximum_fusion
  295.4 1.9 convolution_bitcast_fusion.3
  297.3 1.9 convolution_bitcast_fusion.2
  299.2 1.6 maximum_multiply_fusion
  (45 shorter events, 11.2 us)
Async XLA Ops:
  0.6 1.6 copy-start
  2.2 1.2 copy-start.1
  139.0 0.7 copy-start.3
  143.7 1.0 copy-start.2

commit v2 on v1

--- a/solution.py
+++ b/solution.py
@@ -2,6 +2,7 @@
 
 import jax
 import jax.numpy as jnp
+import numpy as np
 from jax import lax
 from jax.experimental import pallas as pl
 from jax.experimental.pallas import tpu as pltpu
@@ -452,33 +453,162 @@
     )(samples, sketch)
 
 
-def mult(left, right):
-    return jnp.dot(left, right, precision=HI, preferred_element_type=F32)
+def inverse2(a, b, c):
+    r = 1.0 / (a * c - b * b)
+    return c * r, -(b * r), a * r
+
+
+def dots(lefts, rights):
+    total = lefts[0] * rights[0]
+    for left, right in zip(lefts[1:], rights[1:]):
+        total = total + left * right
+    return total
+
+
+def inverse_sym(p):
+    n = len(p)
+    if n == 2:
+        a, b, c = inverse2(p[0][0], p[0][1], p[1][1])
+        return [[a, b], [b, c]]
+    h = n // 2
+    top = inverse_sym([row[:h] for row in p[:h]])
+    cross = [row[h:] for row in p[:h]]
+    t, s = eliminate(top, cross, [row[h:] for row in p[h:]])
+    low = inverse_sym(s)
+    x = [[-dots(t[i], low[j]) for j in range(h)] for i in range(h)]
+    first = [[None] * h for _ in range(h)]
+    for i in range(h):
+        for j in range(i, h):
+            first[i][j] = first[j][i] = top[i][j] - dots(x[i], t[j])
+    return [first[i] + x[i] for i in range(h)] + [[x[i][j] for i in range(h)] + low[j] for j in range(h)]
+
+
+def eliminate(top, cross, corner):
+    h = len(top)
+    t = [[dots(top[i], [cross[k][j] for k in range(h)]) for j in range(h)] for i in range(h)]
+    s = [[None] * h for _ in range(h)]
+    for i in range(h):
+        for j in range(i, h):
+            s[i][j] = s[j][i] = corner[i][j] - dots([cross[k][i] for k in range(h)], [t[k][j] for k in range(h)])
+    return t, s
+
+
+def inverse_factor(ref, start):
+    groups = [ref[start + 8 * g:start + 8 * g + 8, start:start + 128] for g in range(16)]
+    lane = lax.broadcasted_iota(jnp.int32, (8, 128), 1)
+    sub = lax.broadcasted_iota(jnp.int32, (8, 128), 0)
+    wide = (8, 128)
+    for g in range(16):
+        own = groups[g]
+        at = 8 * g
+        inside = (lane >= at) & (lane < at + 8)
+        rows = [jnp.broadcast_to(own[k:k + 1, :], wide) for k in range(8)]
+        if g < 15:
+            p = [[None] * 8 for _ in range(8)]
+            for i in range(8):
+                for j in range(i, 8):
+                    p[i][j] = p[j][i] = jnp.broadcast_to(rows[i][:, at + j:at + j + 1], wide)
+            unit = [jnp.where(inside, jnp.where(lane == at + k, 1.0, 0.0), rows[k]) for k in range(8)]
+            top = inverse_sym([row[:4] for row in p[:4]])
+            t, s = eliminate(top, [row[4:] for row in p[:4]], [row[4:] for row in p[4:]])
+            low = inverse_sym(s)
+            rest = [unit[4 + j] - dots([t[i][j] for i in range(4)], unit[:4]) for j in range(4)]
+            q_low = [dots(low[j], rest) for j in range(4)]
+            q_top = [dots(top[i], unit[:4]) - dots(t[i], q_low) for i in range(4)]
+            q = q_top + q_low
+            for v in range(g + 1, 16):
+                cols = [jnp.broadcast_to(groups[v][:, at + k:at + k + 1], wide) for k in range(8)]
+                base = jnp.where(inside, 0.0, groups[v])
+                groups[v] = base - ((dots(cols[:2], q[:2]) + dots(cols[2:4], q[2:4]))
+                                    + (dots(cols[4:6], q[4:6]) + dots(cols[6:], q[6:])))
+        for k in range(8):
+            row = jnp.broadcast_to(own[k:k + 1, :], wide)
+            pivot = jnp.broadcast_to(row[:, at + k:at + k + 1], wide)
+            inv = 1.0 / pivot
+            col = jnp.broadcast_to(own[:, at + k:at + k + 1], wide)
+            base = jnp.where(lane == at + k, 0.0, own)
+            row = jnp.where(lane == at + k, 1.0, row)
+            own = jnp.where(sub > k, base - col * (row * inv), jnp.where(sub == k, row * lax.rsqrt(pivot), own))
+        ref[start + at:start + at + 8, start:start + 128] = jnp.where(lane <= at + sub, own, 0.0)
+
+
+def factor(m_ref):
+    dot = functools.partial(jnp.dot, precision=HI, preferred_element_type=F32)
+    for k in range(4):
+        at = 128 * k
+        inverse_factor(m_ref, at)
+        w = m_ref[at:at + 128, at:at + 128]
+        if k > 0:
+            m_ref[at:at + 128, :at] = dot(w, m_ref[at:at + 128, :at])
+        if k < 3:
+            u = dot(w, m_ref[at:at + 128, at + 128:])
+            ut = u.T
+            m_ref[at + 128:, at + 128:] = m_ref[at + 128:, at + 128:] - dot(ut, u)
+            if k > 0:
+                m_ref[at + 128:, :at] = m_ref[at + 128:, :at] - dot(ut, m_ref[at:at + 128, :at])
+            m_ref[at + 128:, at:at + 128] = -dot(ut, w)
+            m_ref[at:at + 128, at + 128:] = jnp.zeros((128, 384 - at), F32)
+
+
+def finish_kernel(scale, y_ref, b_ref, g_ref, basis_ref, proj_ref, m_ref, l_hi, l_lo):
+    packed = g_ref[...]
+    row = lax.broadcasted_iota(jnp.int32, (256, 256), 0)
+    col = lax.broadcasted_iota(jnp.int32, (256, 256), 1)
+    turned = packed.T
+    gram_r = jnp.where(row >= col, packed, turned)
+    gram_i = jnp.where(row < col, packed, jnp.where(row > col, -turned, 0.0))
+    m_ref[:256, :256] = gram_r
+    m_ref[256:, 256:] = gram_r
+    m_ref[256:, :256] = gram_i
+    m_ref[:256, 256:] = -gram_i
+    factor(m_ref)
+    for i in range(4):
+        rows = slice(128 * i, 128 * i + 128)
+        l_hi[rows, :], l_lo[rows, :] = split(m_ref[rows, :])
+
+    def product(left_hi, left_lo, right_hi, right_lo):
+        dot = functools.partial(
+            lax.dot_general, dimension_numbers=(((1,), (1,)), ((), ())), preferred_element_type=F32)
+        return dot(left_hi, right_hi) + (dot(left_hi, right_lo) + dot(left_lo, right_hi))
+
+    @pl.loop(0, 2)
+    def _(i):
+        rows = pl.ds(i * 256, 256)
+        real, imag = y_ref[rows, :256], y_ref[rows, 256:]
+        basis_ref[0, rows, :] = product(*split(jnp.concatenate([real, -imag], 1)), l_hi[...], l_lo[...]) * scale
+        basis_ref[1, rows, :] = product(*split(jnp.concatenate([imag, real], 1)), l_hi[...], l_lo[...]) * scale
+
+    @pl.loop(0, 2)
+    def _(i):
+        rows = pl.ds(i * 256, 256)
+        real, imag = b_ref[0], b_ref[1]
+        hi, lo = l_hi[rows, :], l_lo[rows, :]
+        proj_ref[0, rows, :] = product(hi, lo, *split(jnp.concatenate([real, -imag], 1)))
+        proj_ref[1, rows, :] = product(hi, lo, *split(jnp.concatenate([imag, real], 1)))
+
+
+def finish(y, b, packed, scale):
+    vmem = pl.BlockSpec(memory_space=pltpu.VMEM)
+    return pl.pallas_call(
+        functools.partial(finish_kernel, scale),
+        out_shape=(jax.ShapeDtypeStruct((2, 512, 512), F32),) * 2,
+        in_specs=[vmem] * 3,
+        out_specs=(vmem,) * 2,
+        scratch_shapes=[
+            pltpu.VMEM((512, 512), F32),
+            pltpu.VMEM((512, 512), BF16),
+            pltpu.VMEM((512, 512), BF16),
+        ],
+        compiler_params=pltpu.CompilerParams(vmem_limit_bytes=48 * 2**20),
+        name="finish",
+    )(y, b, packed)
 
 
 def per_device(samples, sketch):
     y, b, packed = power(samples, sketch)
-    y = y.reshape(512, 512)
-    b = b.reshape(2, 512, 256)
-    packed = packed.reshape(256, 256)
-    gram_r = jnp.tril(packed) + jnp.tril(packed, -1).T
-    gram_i = jnp.triu(packed, 1) - jnp.triu(packed, 1).T
-    gram = jnp.concatenate(
-        [jnp.concatenate([gram_r, -gram_i], 1), jnp.concatenate([gram_i, gram_r], 1)], 0
-    )
-    lower = jnp.linalg.cholesky(gram)
-    inverse = lax.linalg.triangular_solve(lower, jnp.eye(512, dtype=F32), left_side=True, lower=True)
-    yr, yi = y[:, :256], y[:, 256:]
     total_rows = samples.shape[1] * lax.axis_size("rows")
-    scale = jnp.sqrt(jnp.float32(2 * total_rows))
-    top = mult(jnp.concatenate([yr, -yi], 1), inverse.T)
-    bot = mult(jnp.concatenate([yi, yr], 1), inverse.T)
-    basis = jnp.stack([top, bot]) * scale
-    projected = jnp.stack([
-        mult(inverse, jnp.concatenate([b[0], -b[1]], 1).T),
-        mult(inverse, jnp.concatenate([b[1], b[0]], 1).T),
-    ])
-    return (basis, projected)
+    scale = float(np.sqrt(np.float32(2 * total_rows)))
+    return finish(y.reshape(512, 512), b.reshape(2, 512, 256), packed.reshape(256, 256), scale)
 
 
 def solution(mesh):

time: 305 us -> 206 us (0.68); the launches traced: 301 us -> 206 us
  other arithmetic: 126 us -> 0 us
  Pallas kernels: 135 us -> 202 us
  matrix products: 18.6 us -> 0 us
  local copies, waits for them, and re-layouts: 17.9 us -> 2.81 us
  between operations: 3.81 us -> 0.65 us
    another operation x18 -> x0, other arithmetic: 121 us -> none  [the longest x14 78.8 us: per_device(): lower = jnp.linalg.cholesky(gram)]
    pallas_call x0 -> x1, Pallas kernels: none -> 68.2 us  [finish(): pl.pallas_call(functools.partial(finish_kernel, scale), out_shape=(jax.Sh...]
    another operation x17 -> x0, local copies, waits for them, and re-layouts: 11.8 us -> none
    another operation x13 -> x0, matrix products: 11.1 us -> none  [the longest x7 5.67 us: per_device(): lax.linalg.triangular_solve(lower, jnp.eye(512, dtype=F32), left_side=Tru...]
    dot_general x4 -> x0, matrix products: 7.47 us -> none  [mult(): return jnp.dot(left, right, precision=HI, preferred_element_type=F32)]
where the time goes in v2:
time: 206 us
  Pallas kernels  202 us (98%)
  local copies, waits for them, and re-layouts  2.81 us (1%)
    pallas_call x1, Pallas kernels, power(): pl.pallas_call(power_kernel, out_shape=(jax.ShapeDtypeStruct((8, 2, 32, 5...  134 us
    pallas_call x1, Pallas kernels, finish(): pl.pallas_call(functools.partial(finish_kernel, scale), out_shape=(jax.Sh...  68.2 us

profile of v2, /device:TPU:1, one launch (start us, length us, event | category | flops | bytes accessed | tf_op | source)
XLA Modules:
  0.0 205.8 jit_solution(7189030265042673847)
XLA Ops:
  0.6 0.0 copy-start
  0.6 1.6 copy-done
  2.2 0.0 copy-start.1
  2.2 1.2 copy-done.1
  3.4 134.2 %power.1 = (f32[8,2,32,512]{3,2,1,0:T(8,128)S(1)}, f32[2,2,4,4,16,256]{5,4,3,2,1,0:T(8,128)S(1)}, f32[2,4,4,8,256]{4,3,2,1,0:T(8,128)S(1)}) custom-call(f32[2,512,512]{2,1,0:T(8,128)S(1)} %copy-done, f32[2,512,256]{2,1,0:T(8,128)S(1)} %copy-done.1), custom_call_target="tpu_custom_call" | custom-call | tf_op jit(solution)/shard_map/power/pallas_call | solution.py:427
  137.6 68.2 %finish.1 = (f32[2,512,512]{2,1,0:T(8,128)}, f32[2,512,512]{2,1,0:T(8,128)}) custom-call(f32[512,512]{1,0:T(8,128)S(1)} %bitcast.3, f32[2,512,256]{2,1,0:T(8,128)S(1)} %bitcast.4, f32[256,256]{1,0:T(8,128)S(1)} %bitcast.5), custom_call_target="tpu_custom_call" | custom-call | tf_op jit(solution)/shard_map/finish/pallas_call | solution.py:592
Async XLA Ops:
  0.6 1.6 copy-start
  2.2 1.2 copy-start.1

commit v3 on v1

--- a/solution.py
+++ b/solution.py
@@ -2,6 +2,7 @@
 
 import jax
 import jax.numpy as jnp
+import numpy as np
 from jax import lax
 from jax.experimental import pallas as pl
 from jax.experimental.pallas import tpu as pltpu
@@ -325,10 +326,133 @@
             tile(i, j)
 
 
-def power_kernel(a_ref, s_ref, y_ref, b_ref, g_ref, x_hi, x_lo, xt_hi, xt_lo, t_hi, t_lo,
+def dots(lefts, rights):
+    terms = [left * right for left, right in zip(lefts, rights)]
+    while len(terms) > 1:
+        terms = [sum(terms[i + 1:i + 2], terms[i]) for i in range(0, len(terms), 2)]
+    return terms[0]
+
+
+def inverse_factor(ref, start, hook):
+    groups = [ref[start + 8 * g:start + 8 * g + 8, start:start + 128] for g in range(16)]
+    wide = (8, 128)
+    lane = lax.broadcasted_iota(jnp.int32, wide, 1)
+    sub = lax.broadcasted_iota(jnp.int32, wide, 0)
+
+    def row(value, k):
+        return jnp.broadcast_to(value[k:k + 1, :], wide)
+
+    def col(value, k):
+        return jnp.broadcast_to(value[:, k:k + 1], wide)
+
+    for g in range(16):
+        at = 8 * g
+        inside = (lane >= at) & (lane < at + 8)
+        own = groups[g]
+        c = [col(own, at + k) for k in range(8)]
+        u = jnp.where(inside, jnp.where(lane == at + sub, 1.0, 0.0), own)
+        inverse = root = jnp.zeros(wide, F32)
+        for k in range(8):
+            pivot = row(c[k], k)
+            inv = 1.0 / pivot
+            inverse = jnp.where(sub == k, inv, inverse)
+            root = jnp.where(sub == k, lax.rsqrt(pivot), root)
+            if k < 7:
+                f = jnp.where(sub > k, c[k], 0.0) * inv
+                for m in range(k + 1, 8):
+                    c[m] = c[m] - f * row(c[m], k)
+                u = u - f * row(u, k)
+        ref[start + at:start + at + 8, start:start + 128] = jnp.where(lane <= at + sub, u * root, 0.0)
+        hook((start + at) // 8)
+        if g == 15:
+            break
+        q = u * inverse
+        for m in range(7, 0, -1):
+            q = q - jnp.where(sub < m, c[m] * inverse, 0.0) * row(q, m)
+        rows = [row(q, k) for k in range(8)]
+        for v in range(g + 1, 16):
+            cols = [col(groups[v], at + k) for k in range(8)]
+            groups[v] = jnp.where(inside, 0.0, groups[v]) - dots(cols, rows)
+
+
+def factor(m_ref, hook):
+    dot = functools.partial(jnp.dot, precision=HI, preferred_element_type=F32)
+    for k in range(4):
+        at = 128 * k
+        inverse_factor(m_ref, at, hook)
+        w = m_ref[at:at + 128, at:at + 128]
+        if k > 0:
+            m_ref[at:at + 128, :at] = dot(w, m_ref[at:at + 128, :at])
+        if k < 3:
+            u = dot(w, m_ref[at:at + 128, at + 128:])
+            ut = u.T
+            m_ref[at + 128:, at + 128:] = m_ref[at + 128:, at + 128:] - dot(ut, u)
+            if k > 0:
+                m_ref[at + 128:, :at] = m_ref[at + 128:, :at] - dot(ut, m_ref[at:at + 128, :at])
+            m_ref[at + 128:, at:at + 128] = -dot(ut, w)
+            m_ref[at:at + 128, at + 128:] = jnp.zeros((128, 384 - at), F32)
+
+
+def set_gram(packed, m_ref):
+    row = lax.broadcasted_iota(jnp.int32, (256, 256), 0)
+    col = lax.broadcasted_iota(jnp.int32, (256, 256), 1)
+    turned = packed.T
+    gram_r = jnp.where(row >= col, packed, turned)
+    gram_i = jnp.where(row < col, packed, jnp.where(row > col, -turned, 0.0))
+    m_ref[:256, :256] = gram_r
+    m_ref[256:, 256:] = gram_r
+    m_ref[256:, :256] = gram_i
+    m_ref[:256, 256:] = -gram_i
+
+
+def finish_kernel(scale, y_ref, b_ref, m_ref, basis_ref, proj_ref, l_hi, l_lo):
+    for i in range(4):
+        rows = slice(128 * i, 128 * i + 128)
+        l_hi[rows, :], l_lo[rows, :] = split(m_ref[rows, :])
+
+    def product(left_hi, left_lo, right_hi, right_lo):
+        dot = functools.partial(
+            lax.dot_general, dimension_numbers=(((1,), (1,)), ((), ())), preferred_element_type=F32)
+        return dot(left_hi, right_hi) + (dot(left_hi, right_lo) + dot(left_lo, right_hi))
+
+    @pl.loop(0, 2)
+    def _(i):
+        rows = pl.ds(i * 256, 256)
+        real, imag = y_ref[rows, :256], y_ref[rows, 256:]
+        basis_ref[0, rows, :] = product(*split(jnp.concatenate([real, -imag], 1)), l_hi[...], l_lo[...]) * scale
+        basis_ref[1, rows, :] = product(*split(jnp.concatenate([imag, real], 1)), l_hi[...], l_lo[...]) * scale
+
+    @pl.loop(0, 2)
+    def _(i):
+        rows = pl.ds(i * 256, 256)
+        real, imag = b_ref[0], b_ref[1]
+        hi, lo = l_hi[rows, :], l_lo[rows, :]
+        proj_ref[0, rows, :] = product(hi, lo, *split(jnp.concatenate([real, -imag], 1)))
+        proj_ref[1, rows, :] = product(hi, lo, *split(jnp.concatenate([imag, real], 1)))
+
+
+def finish(y, b, inverse, scale):
+    vmem = pl.BlockSpec(memory_space=pltpu.VMEM)
+    return pl.pallas_call(
+        functools.partial(finish_kernel, scale),
+        out_shape=(jax.ShapeDtypeStruct((2, 512, 512), F32),) * 2,
+        in_specs=[vmem] * 3,
+        out_specs=(vmem,) * 2,
+        scratch_shapes=[
+            pltpu.VMEM((512, 512), BF16),
+            pltpu.VMEM((512, 512), BF16),
+        ],
+        compiler_params=pltpu.CompilerParams(vmem_limit_bytes=48 * 2**20),
+        name="finish",
+    )(y, b, inverse)
+
+HOOKS = (0, 4, 11, 18, 25, 33, 41, 50)
+
+
+def power_kernel(a_ref, s_ref, y_ref, b_ref, m_ref, x_hi, x_lo, xt_hi, xt_lo, t_hi, t_lo,
                  z_part, z_slots, z_full, z_part2, z_slots2,
                  r_part, r_core, r_line, r_point, r_full, r_part2, r_core2, r_line2, r_point2,
-                 g_part, g_core, g_line, g_point, g_z, send_sem, recv_sem):
+                 g_ref, g_part, g_core, g_line, g_point, g_z, send_sem, recv_sem):
     place = Place()
     greet(place)
     copies = Copies(send_sem, recv_sem)
@@ -403,12 +527,32 @@
     low = lax.broadcasted_iota(jnp.int32, (256, 256), 0) >= lax.broadcasted_iota(jnp.int32, (256, 256), 1)
     g_part[...] = jnp.where(low, gram_r, gram_i).reshape(2, 4, 4, 8, 256)
     gram_steps = SumAll(place, copies, 2 * Z_SLOTS + ROW_SLOTS, g_part, g_core, g_line, g_point, g_z, g_ref).steps()
-    interleave(gram_steps, steps)
-
-    chunks_to_t(y_ref)
-    multiply(xt_hi, xt_lo, t_hi, t_lo, store_rows(r_part2))
-    run(SumRows(place, copies, 2 * Z_SLOTS + ROW_SLOTS + GRAM_SLOTS, r_part2, r_core2, r_line2, r_point2,
-                b_ref).steps())
+    for _ in range(4):
+        next(gram_steps)
+    next(steps)
+    next(gram_steps)
+    next(steps)
+    next(gram_steps)
+    next(steps)
+    run(gram_steps)
+
+    def behind():
+        run(steps)
+        chunks_to_t(y_ref)
+        multiply(xt_hi, xt_lo, t_hi, t_lo, store_rows(r_part2))
+        yield
+        yield from SumRows(place, copies, 2 * Z_SLOTS + ROW_SLOTS + GRAM_SLOTS, r_part2, r_core2, r_line2,
+                           r_point2, b_ref).steps()
+
+    rest = behind()
+
+    def hook(done):
+        if done in HOOKS:
+            next(rest)
+
+    set_gram(g_ref[...].reshape(256, 256), m_ref)
+    factor(m_ref, hook)
+    run(rest)
     copies.finish()
 
 
@@ -428,7 +572,7 @@
         out_shape=(
             jax.ShapeDtypeStruct((8, 2, 32, 512), F32),
             jax.ShapeDtypeStruct((2, 2, 4, 4, 16, 256), F32),
-            jax.ShapeDtypeStruct((2, 4, 4, 8, 256), F32),
+            jax.ShapeDtypeStruct((512, 512), F32),
         ),
         in_specs=[vmem] * 2,
         out_specs=(vmem,) * 3,
@@ -437,7 +581,7 @@
             *[pltpu.VMEM((1024, 512), BF16)] * 2,
             chunks, boxes, chunks, chunks, boxes,
             *rows, pltpu.VMEM((2, 2, 4, 4, 16, 256), F32), *rows,
-            pltpu.VMEM((2, 4, 4, 8, 256), F32),
+            *[pltpu.VMEM((2, 4, 4, 8, 256), F32)] * 2,
             pltpu.VMEM((4, 4, 8, 256), F32),
             pltpu.VMEM((3, 4, 8, 256), F32),
             pltpu.VMEM((3, 8, 256), F32),
@@ -452,33 +596,11 @@
     )(samples, sketch)
 
 
-def mult(left, right):
-    return jnp.dot(left, right, precision=HI, preferred_element_type=F32)
-
-
 def per_device(samples, sketch):
-    y, b, packed = power(samples, sketch)
-    y = y.reshape(512, 512)
-    b = b.reshape(2, 512, 256)
-    packed = packed.reshape(256, 256)
-    gram_r = jnp.tril(packed) + jnp.tril(packed, -1).T
-    gram_i = jnp.triu(packed, 1) - jnp.triu(packed, 1).T
-    gram = jnp.concatenate(
-        [jnp.concatenate([gram_r, -gram_i], 1), jnp.concatenate([gram_i, gram_r], 1)], 0
-    )
-    lower = jnp.linalg.cholesky(gram)
-    inverse = lax.linalg.triangular_solve(lower, jnp.eye(512, dtype=F32), left_side=True, lower=True)
-    yr, yi = y[:, :256], y[:, 256:]
+    y, b, inverse = power(samples, sketch)
     total_rows = samples.shape[1] * lax.axis_size("rows")
-    scale = jnp.sqrt(jnp.float32(2 * total_rows))
-    top = mult(jnp.concatenate([yr, -yi], 1), inverse.T)
-    bot = mult(jnp.concatenate([yi, yr], 1), inverse.T)
-    basis = jnp.stack([top, bot]) * scale
-    projected = jnp.stack([
-        mult(inverse, jnp.concatenate([b[0], -b[1]], 1).T),
-        mult(inverse, jnp.concatenate([b[1], b[0]], 1).T),
-    ])
-    return (basis, projected)
+    scale = float(np.sqrt(np.float32(2 * total_rows)))
+    return finish(y.reshape(512, 512), b.reshape(2, 512, 256), inverse, scale)
 
 
 def solution(mesh):

time: 305 us -> 146 us (0.48); the launches traced: 301 us -> 146 us
  other arithmetic: 126 us -> 0 us
  matrix products: 18.6 us -> 0 us
  local copies, waits for them, and re-layouts: 17.9 us -> 1.22 us
  Pallas kernels: 135 us -> 144 us
  between operations: 3.81 us -> 0.65 us
    another operation x18 -> x0, other arithmetic: 121 us -> none  [the longest x14 78.8 us: per_device(): lower = jnp.linalg.cholesky(gram)]
    another operation x17 -> x0, local copies, waits for them, and re-layouts: 11.8 us -> none
    another operation x13 -> x0, matrix products: 11.1 us -> none  [the longest x7 5.67 us: per_device(): lax.linalg.triangular_solve(lower, jnp.eye(512, dtype=F32), left_side=Tru...]
    dot_general x4 -> x0, matrix products: 7.47 us -> none  [mult(): return jnp.dot(left, right, precision=HI, preferred_element_type=F32)]
    pallas_call x0 -> x1, Pallas kernels: none -> 5.99 us  [finish(): pl.pallas_call(functools.partial(finish_kernel, scale), out_shape=(jax.Sh...]
    unnamed x8 -> x2, local copies, waits for them, and re-layouts: 4.46 us -> 1.22 us
    pallas_call x1, Pallas kernels: 135 us -> 138 us  [power(): pl.pallas_call(power_kernel, out_shape=(jax.ShapeDtypeStruct((8, 2, 32, 5...]
where the time goes in v3:
time: 146 us
  Pallas kernels  144 us (99%)
    pallas_call x1, Pallas kernels, power(): pl.pallas_call(power_kernel, out_shape=(jax.ShapeDtypeStruct((8, 2, 32, 5...  138 us
    pallas_call x1, Pallas kernels, finish(): pl.pallas_call(functools.partial(finish_kernel, scale), out_shape=(jax.Sh...  5.99 us

profile of v3, /device:TPU:1, one launch (start us, length us, event | category | flops | bytes accessed | tf_op | source)
XLA Modules:
  0.0 145.6 jit_solution(10475817913545863879)
XLA Ops:
  0.6 0.0 copy-start
  0.6 1.2 copy-done
  1.9 137.7 %power.1 = (f32[8,2,32,512]{3,2,1,0:T(8,128)S(1)}, f32[2,2,4,4,16,256]{5,4,3,2,1,0:T(8,128)S(1)}, f32[512,512]{1,0:T(8,128)S(1)}) custom-call(f32[2,512,512]{2,1,0:T(8,128)} %a_ref.1, f32[2,512,256]{2,1,0:T(8,128)S(1)} %copy-done), custom_call_target="tpu_custom_call" | custom-call | tf_op jit(solution)/shard_map/power/pallas_call | solution.py:570
  139.6 6.0 %finish.1 = (f32[2,512,512]{2,1,0:T(8,128)}, f32[2,512,512]{2,1,0:T(8,128)}) custom-call(f32[512,512]{1,0:T(8,128)S(1)} %bitcast.2, f32[2,512,256]{2,1,0:T(8,128)S(1)} %bitcast.3, f32[512,512]{1,0:T(8,128)S(1)} %get-tuple-element.7.m_ref), custom_call_target="tpu_custom_call" | custom-call | tf_op jit(solution)/shard_map/finish/pallas_call | solution.py:436
Async XLA Ops:
  0.6 1.2 copy-start

commit v4 on v3

--- a/solution.py
+++ b/solution.py
@@ -13,8 +13,8 @@
 F32 = jnp.float32
 BF16 = jnp.bfloat16
 
-Z_SLOTS = 28
-ROW_SLOTS = 34
+Z_SLOTS = 56
+ROW_SLOTS = 68
 GRAM_SLOTS = 21
 
 
@@ -79,7 +79,7 @@
     peers += [place.along_z(d) for d in range(1, 8)]
     for peer in peers:
         pl.semaphore_signal(barrier, inc=1, device_id=peer, device_id_type=MESH)
-    pl.semaphore_wait(barrier, len(peers))
+    return lambda: pl.semaphore_wait(barrier, len(peers))
 
 
 def wrap8(value):
@@ -91,150 +91,146 @@
         self.place, self.copies, self.base = place, copies, base
         self.part, self.slots, self.full = part, slots, full
 
+    @staticmethod
+    def box(way, quarter, dist):
+        lead = (way > 0) == (quarter < 2)
+        return (0 if way > 0 else 14) + (quarter % 2) * 7 + (dist - 1 if lead else 3 + dist)
+
+    def push(self, way, quarter, dist):
+        box = self.box(way, quarter, dist)
+        chunk = wrap8(self.place.z + way * dist)
+        self.copies.send(self.base + box, self.part.at[chunk, quarter], self.slots.at[box],
+                         self.place.along_z(way))
+
+    def pull(self, way, quarter, dist):
+        box = self.box(way, quarter, dist)
+        self.copies.arrived(self.base + box)
+        chunk = wrap8(self.place.z + way * (dist - 1))
+        self.part[chunk, quarter] = self.part[chunk, quarter] + self.slots[box]
+
+    LEADS = ((1, 0), (-1, 2), (1, 1), (-1, 3))
+    OTHERS = ((1, 2), (-1, 0), (1, 3), (-1, 1))
+
     def scatter_steps(self):
-        place, copies, part, slots = self.place, self.copies, self.part, self.slots
-
-        def slot(way, half, dist):
-            return self.base + (0 if way > 0 else 7) + (dist - 1 if half == lead(way) else 3 + dist)
-
-        def lead(way):
-            return 0 if way > 0 else 1
-
-        def box(way, half, dist):
-            return (0 if way > 0 else 7) + (dist - 1 if half == lead(way) else 3 + dist)
-
-        def push(way, half, dist):
-            chunk = wrap8(place.z + way * dist)
-            copies.send(slot(way, half, dist), part.at[chunk, half], slots.at[box(way, half, dist)],
-                        place.along_z(way))
-
-        def pull(way, half, dist):
-            copies.arrived(slot(way, half, dist))
-            chunk = wrap8(place.z + way * (dist - 1))
-            part[chunk, half] = part[chunk, half] + slots[box(way, half, dist)]
-
-        for way in (1, -1):
-            push(way, lead(way), 4)
-        for way in (1, -1):
-            push(way, 1 - lead(way), 3)
+        for way, quarter in self.LEADS:
+            self.push(way, quarter, 4)
+        yield
+        for way, quarter in self.OTHERS:
+            self.push(way, quarter, 3)
         yield
         for step in range(3):
-            for way in (1, -1):
-                half = lead(way)
-                pull(way, half, 4 - step)
-                push(way, half, 3 - step)
-            for way in (1, -1):
-                half = 1 - lead(way)
-                pull(way, half, 3 - step)
+            for way, quarter in self.LEADS:
+                self.pull(way, quarter, 4 - step)
+                self.push(way, quarter, 3 - step)
+            for way, quarter in self.OTHERS:
+                self.pull(way, quarter, 3 - step)
                 if step < 2:
-                    push(way, half, 2 - step)
+                    self.push(way, quarter, 2 - step)
             yield
-        for way in (1, -1):
-            pull(way, lead(way), 1)
+        for way, quarter in self.LEADS:
+            self.pull(way, quarter, 1)
         yield
 
     def gather_steps(self):
-        place, copies, full, part = self.place, self.copies, self.full, self.part
-        me = place.z
-        full[me] = part[me]
-        base = self.base + 14
-
-        def slot(way, half, dist):
-            return base + (0 if way > 0 else 7) + (dist * 2 + half if dist < 3 else 6)
-
-        def push(way, half, dist):
-            chunk = wrap8(me - way * dist)
-            ref = full.at[chunk, half]
-            copies.send(slot(way, half, dist), ref, ref, place.along_z(way))
-
-        for half in (0, 1):
-            for way in (1, -1):
-                push(way, half, 0)
+        place, copies, full = self.place, self.copies, self.full
+        full[place.z] = self.part[place.z]
+        base = self.base + 28
+
+        def slot(way, quarter, dist):
+            return base + (0 if way > 0 else 14) + (quarter * 3 + dist if dist < 3 else 12 + quarter % 2)
+
+        def push(way, quarter, dist):
+            chunk = wrap8(place.z - way * dist)
+            ref = full.at[chunk, quarter]
+            copies.send(slot(way, quarter, dist), ref, ref, place.along_z(way))
+
+        order = self.LEADS + self.OTHERS
+        for way, quarter in order:
+            push(way, quarter, 0)
         yield
         for dist in (1, 2):
-            for half in (0, 1):
-                for way in (1, -1):
-                    copies.arrived(slot(way, half, dist - 1))
-                    push(way, half, dist)
+            for way, quarter in order:
+                copies.arrived(slot(way, quarter, dist - 1))
+                push(way, quarter, dist)
             yield
-        for half in (0, 1):
-            for way in (1, -1):
-                copies.arrived(slot(way, half, 2))
-                if half == (0 if way > 0 else 1):
-                    push(way, half, 3)
-        yield
-        for way in (1, -1):
-            copies.arrived(slot(way, 0 if way > 0 else 1, 3))
+        for way, quarter in self.LEADS:
+            copies.arrived(slot(way, quarter, 2))
+            push(way, quarter, 3)
+        for way, quarter in self.OTHERS:
+            copies.arrived(slot(way, quarter, 2))
+        yield
+        for way, quarter in self.LEADS:
+            copies.arrived(slot(way, quarter, 3))
         yield
 
 
 class SumRows:
+    STREAMS = ((0, 0), (1, 0), (0, 1), (1, 1))
+
     def __init__(self, place, copies, base, part, from_core, from_line, from_point, full):
         self.place, self.copies, self.base = place, copies, base
         self.part, self.full = part, full
         self.from_core, self.from_line, self.from_point = from_core, from_line, from_point
 
+    def slot(self, h, s, kind, d):
+        return self.base + 17 * (2 * h + s) + kind + d
+
     def steps(self):
-        place, copies, base = self.place, self.copies, self.base
+        place, copies, slot = self.place, self.copies, self.slot
         part, full, core = self.part, self.full, place.core
         first = [place.at(0), place.at(1)]
         second = [place.at(1), place.at(0)]
-        for h in (0, 1):
-            copies.send(base + h, part.at[h, 1 - core], self.from_core.at[h], place.sibling())
-        yield
-        base += 2
-        for h in (0, 1):
-            copies.arrived(base - 2 + h)
-            for d in (2, 1, 3):
+        CORE, LINE, POINT, POINT_BACK, LINE_BACK, BACK = 0, 0, 3, 6, 9, 13
+        for h, s in self.STREAMS:
+            copies.send(slot(h, s, CORE, 0), part.at[h, 1 - core, s], self.from_core.at[h, s], place.sibling())
+        yield
+        for h, s in self.STREAMS:
+            copies.arrived(slot(h, s, CORE, 0))
+            for d in (2, 1, 3, 0):
                 at = lax.rem(first[h] + d, 4)
-                part[h, core, at] = part[h, core, at] + self.from_core[h, at]
-                copies.send(base + 3 * h + d - 1, part.at[h, core, at], self.from_line.at[h, d - 1],
-                            place.line(h, d))
-            at = first[h]
-            part[h, core, at] = part[h, core, at] + self.from_core[h, at]
-        yield
-        base += 6
-        for h in (0, 1):
+                part[h, core, s, at] = part[h, core, s, at] + self.from_core[h, s, at]
+                if d:
+                    copies.send(slot(h, s, LINE, d), part.at[h, core, s, at], self.from_line.at[h, s, d - 1],
+                                place.line(h, d))
+        yield
+        for h, s in self.STREAMS:
             a = first[h]
             for d in (1, 2, 3):
-                copies.arrived(base - 6 + 3 * h + d - 1)
-            part[h, core, a] = (part[h, core, a] + self.from_line[h, 0]) + (
-                self.from_line[h, 1] + self.from_line[h, 2])
+                copies.arrived(slot(h, s, LINE, d))
+            part[h, core, s, a] = (part[h, core, s, a] + self.from_line[h, s, 0]) + (
+                self.from_line[h, s, 1] + self.from_line[h, s, 2])
             for d in (2, 1, 3):
                 b = lax.rem(second[h] + d, 4)
-                copies.send(base + 3 * h + d - 1, part.at[h, core, a, b], self.from_point.at[h, d - 1],
+                copies.send(slot(h, s, POINT, d), part.at[h, core, s, a, b], self.from_point.at[h, s, d - 1],
                             place.line(1 - h, d))
         yield
-        base += 6
-        for h in (0, 1):
+        for h, s in self.STREAMS:
             a, b = first[h], second[h]
             for d in (1, 2, 3):
-                copies.arrived(base - 6 + 3 * h + d - 1)
-            full[h, core, a, b] = (part[h, core, a, b] + self.from_point[h, 0]) + (
-                self.from_point[h, 1] + self.from_point[h, 2])
+                copies.arrived(slot(h, s, POINT, d))
+            full[h, core, s, a, b] = (part[h, core, s, a, b] + self.from_point[h, s, 0]) + (
+                self.from_point[h, s, 1] + self.from_point[h, s, 2])
+            ref = full.at[h, core, s, a, b]
             for d in (2, 1, 3):
-                ref = full.at[h, core, a, b]
-                copies.send(base + 3 * h + d - 1, ref, ref, place.line(1 - h, d))
-        yield
-        base += 6
-        for h in (0, 1):
-            a = first[h]
+                copies.send(slot(h, s, POINT_BACK, d), ref, ref, place.line(1 - h, d))
+        yield
+        for h, s in self.STREAMS:
             for d in (1, 2, 3):
-                copies.arrived(base - 6 + 3 * h + d - 1)
-            ref = full.at[h, core, a]
+                copies.arrived(slot(h, s, POINT_BACK, d))
+            ref = full.at[h, core, s, first[h]]
             for d in (2, 1, 3):
-                copies.send(base + 3 * h + d - 1, ref, ref, place.line(h, d))
-            copies.send(base + 6 + 4 * h, ref, ref, place.sibling())
-        yield
-        for h in (0, 1):
+                copies.send(slot(h, s, LINE_BACK, d), ref, ref, place.line(h, d))
+            copies.send(slot(h, s, BACK, 0), ref, ref, place.sibling())
+        yield
+        for h, s in self.STREAMS:
             for d in (1, 3, 2):
-                copies.arrived(base + 3 * h + d - 1)
-                ref = full.at[h, core, lax.rem(first[h] - d + 4, 4)]
-                copies.send(base + 6 + 4 * h + d, ref, ref, place.sibling())
-        yield
-        for h in (0, 1):
+                copies.arrived(slot(h, s, LINE_BACK, d))
+                ref = full.at[h, core, s, lax.rem(first[h] - d + 4, 4)]
+                copies.send(slot(h, s, BACK, d), ref, ref, place.sibling())
+        yield
+        for h, s in self.STREAMS:
             for d in range(4):
-                copies.arrived(base + 6 + 4 * h + d)
+                copies.arrived(slot(h, s, BACK, d))
         yield
 
 
@@ -312,18 +308,14 @@
         live = [one for one in live if next(one, run) is None]
 
 
-def multiply(x_hi, x_lo, t_hi, t_lo, store):
-    def tile(i, j):
-        rows, lanes = pl.ds(i * 256, 256), pl.ds(j * 256, 256)
+def multiply(x_hi, x_lo, t_hi, t_lo, store, i):
+    rows = pl.ds(pl.multiple_of(i * 256, 256), 256)
+    dot = functools.partial(jnp.dot, preferred_element_type=F32)
+    for j in range(2):
+        lanes = pl.ds(j * 256, 256)
         xh, xl = x_hi[rows, :], x_lo[rows, :]
         th, tl = t_hi[:, lanes], t_lo[:, lanes]
-        dot = functools.partial(jnp.dot, preferred_element_type=F32)
         store(i, j, dot(xh, th) + (dot(xh, tl) + dot(xl, th)))
-
-    @pl.loop(0, 2)
-    def _(i):
-        for j in range(2):
-            tile(i, j)
 
 
 def dots(lefts, rights):
@@ -446,15 +438,15 @@
         name="finish",
     )(y, b, inverse)
 
-HOOKS = (0, 4, 11, 18, 25, 33, 41, 50)
-
-
-def power_kernel(a_ref, s_ref, y_ref, b_ref, m_ref, x_hi, x_lo, xt_hi, xt_lo, t_hi, t_lo,
+HOOKS = (0, 8, 16, 24, 32, 42, 50)
+
+
+def power_kernel(a_hbm, s_hbm, y_ref, b_ref, m_ref, x_hi, x_lo, xt_hi, xt_lo, t_hi, t_lo,
                  z_part, z_slots, z_full, z_part2, z_slots2,
                  r_part, r_core, r_line, r_point, r_full, r_part2, r_core2, r_line2, r_point2,
-                 g_ref, g_part, g_core, g_line, g_point, g_z, send_sem, recv_sem):
+                 g_ref, g_part, g_core, g_line, g_point, g_z, a_ref, s_ref, in_sem, send_sem, recv_sem):
     place = Place()
-    greet(place)
+    all_here = greet(place)
     copies = Copies(send_sem, recv_sem)
 
     def set_pair(rows, real, imag, sign):
@@ -466,26 +458,44 @@
         ):
             t_hi[at, lanes], t_lo[at, lanes] = split(value)
 
+    fetches = [
+        pltpu.make_async_copy(src, dst, in_sem.at[n])
+        for n, (src, dst) in enumerate(((s_hbm, s_ref), (a_hbm, a_ref)))
+    ]
+    for fetch in fetches:
+        fetch.start()
+    fetches[0].wait()
+
+    @pl.loop(0, 8)
+    def _(i):
+        rows = pl.ds(i * 64, 64)
+        set_pair(i * 64, s_ref[0, rows, :], s_ref[1, rows, :], -1.0)
+
+    fetches[1].wait()
+
     @pl.loop(0, 8)
     def _(i):
         rows = pl.ds(i * 64, 64)
         for p in (0, 1):
             x_hi[rows, p * 512:(p + 1) * 512], x_lo[rows, p * 512:(p + 1) * 512] = split(a_ref[p, rows, :])
-        set_pair(i * 64, s_ref[0, rows, :], s_ref[1, rows, :], -1.0)
 
     def store_chunks(ref):
         def store(i, j, tile):
-            ref[pl.ds(i * 4, 4), :, :, j * 256:(j + 1) * 256] = tile.reshape(4, 2, 32, 256)
+            ref[pl.ds(i * 4, 4), :, :, j * 256:(j + 1) * 256] = tile.reshape(4, 4, 16, 256)
         return store
 
     def store_rows(ref):
         def store(i, j, tile):
-            ref[j, i] = tile.reshape(4, 4, 16, 256)
+            ref[j, i] = tile.reshape(2, 4, 4, 8, 256)
         return store
 
-    multiply(x_hi, x_lo, t_hi, t_lo, store_chunks(z_part))
+    far = 1 - place.z // 4
     ring = RingZ(place, copies, 0, z_part, z_slots, z_full)
     steps = ring.scatter_steps()
+    multiply(x_hi, x_lo, t_hi, t_lo, store_chunks(z_part), far)
+    all_here()
+    next(steps)
+    multiply(x_hi, x_lo, t_hi, t_lo, store_chunks(z_part), 1 - far)
     next(steps)
 
     @pl.loop(0, 4)
@@ -506,17 +516,25 @@
             set_pair(i * 64, value[:, :256], value[:, 256:], 1.0)
 
     chunks_to_t(z_full)
-    multiply(xt_hi, xt_lo, t_hi, t_lo, store_rows(r_part))
-    run(SumRows(place, copies, Z_SLOTS, r_part, r_core, r_line, r_point, r_full).steps())
+    multiply(xt_hi, xt_lo, t_hi, t_lo, store_rows(r_part), 1 - place.core)
+    steps = SumRows(place, copies, Z_SLOTS, r_part, r_core, r_line, r_point, r_full).steps()
+    next(steps)
+    multiply(xt_hi, xt_lo, t_hi, t_lo, store_rows(r_part), place.core)
+    run(steps)
 
     for k in (0, 1):
-        @pl.loop(0, 4)
-        def _(i):
-            set_pair(k * 256 + i * 64, r_full[0, k, i].reshape(64, 256), r_full[1, k, i].reshape(64, 256), -1.0)
-
-    multiply(x_hi, x_lo, t_hi, t_lo, store_chunks(z_part2))
+        for s in (0, 1):
+            @pl.loop(0, 2)
+            def _(i):
+                at, lines = k * 256 + s * 128 + i * 64, pl.ds(i * 2, 2)
+                set_pair(at, r_full[0, k, s, lines].reshape(64, 256), r_full[1, k, s, lines].reshape(64, 256), -1.0)
+
     ring = RingZ(place, copies, Z_SLOTS + ROW_SLOTS, z_part2, z_slots2, y_ref)
-    run(ring.scatter_steps())
+    steps = ring.scatter_steps()
+    multiply(x_hi, x_lo, t_hi, t_lo, store_chunks(z_part2), far)
+    next(steps)
+    multiply(x_hi, x_lo, t_hi, t_lo, store_chunks(z_part2), 1 - far)
+    run(steps)
     mine = z_part2[place.z].reshape(64, 512)
     steps = ring.gather_steps()
     next(steps)
@@ -539,10 +557,13 @@
     def behind():
         run(steps)
         chunks_to_t(y_ref)
-        multiply(xt_hi, xt_lo, t_hi, t_lo, store_rows(r_part2))
-        yield
-        yield from SumRows(place, copies, 2 * Z_SLOTS + ROW_SLOTS + GRAM_SLOTS, r_part2, r_core2, r_line2,
-                           r_point2, b_ref).steps()
+        multiply(xt_hi, xt_lo, t_hi, t_lo, store_rows(r_part2), 1 - place.core)
+        tail = SumRows(place, copies, 2 * Z_SLOTS + ROW_SLOTS + GRAM_SLOTS, r_part2, r_core2, r_line2,
+                       r_point2, b_ref).steps()
+        next(tail)
+        multiply(xt_hi, xt_lo, t_hi, t_lo, store_rows(r_part2), place.core)
+        yield
+        yield from tail
 
     rest = behind()
 
@@ -559,38 +580,40 @@
 def power(samples, sketch):
     vmem = pl.BlockSpec(memory_space=pltpu.VMEM)
     slots = 2 * Z_SLOTS + 2 * ROW_SLOTS + GRAM_SLOTS
-    chunks = pltpu.VMEM((8, 2, 32, 512), F32)
-    boxes = pltpu.VMEM((14, 32, 512), F32)
+    chunks = pltpu.VMEM((8, 4, 16, 512), F32)
+    boxes = pltpu.VMEM((28, 16, 512), F32)
     rows = [
-        pltpu.VMEM((2, 2, 4, 4, 16, 256), F32),
-        pltpu.VMEM((2, 4, 4, 16, 256), F32),
-        pltpu.VMEM((2, 3, 4, 16, 256), F32),
-        pltpu.VMEM((2, 3, 16, 256), F32),
+        pltpu.VMEM((2, 2, 2, 4, 4, 8, 256), F32),
+        pltpu.VMEM((2, 2, 4, 4, 8, 256), F32),
+        pltpu.VMEM((2, 2, 3, 4, 8, 256), F32),
+        pltpu.VMEM((2, 2, 3, 8, 256), F32),
     ]
     return pl.pallas_call(
         power_kernel,
         out_shape=(
-            jax.ShapeDtypeStruct((8, 2, 32, 512), F32),
-            jax.ShapeDtypeStruct((2, 2, 4, 4, 16, 256), F32),
+            jax.ShapeDtypeStruct((8, 4, 16, 512), F32),
+            jax.ShapeDtypeStruct((2, 2, 2, 4, 4, 8, 256), F32),
             jax.ShapeDtypeStruct((512, 512), F32),
         ),
-        in_specs=[vmem] * 2,
+        in_specs=[pl.BlockSpec(memory_space=pl.ANY)] * 2,
         out_specs=(vmem,) * 3,
         scratch_shapes=[
             *[pltpu.VMEM((512, 1024), BF16)] * 4,
             *[pltpu.VMEM((1024, 512), BF16)] * 2,
             chunks, boxes, chunks, chunks, boxes,
-            *rows, pltpu.VMEM((2, 2, 4, 4, 16, 256), F32), *rows,
+            *rows, pltpu.VMEM((2, 2, 2, 4, 4, 8, 256), F32), *rows,
             *[pltpu.VMEM((2, 4, 4, 8, 256), F32)] * 2,
             pltpu.VMEM((4, 4, 8, 256), F32),
             pltpu.VMEM((3, 4, 8, 256), F32),
             pltpu.VMEM((3, 8, 256), F32),
             pltpu.VMEM((8, 8, 256), F32),
-            pltpu.SemaphoreType.DMA((slots,)),
-            pltpu.SemaphoreType.DMA((slots,)),
+            pltpu.VMEM((2, 512, 512), F32),
+            pltpu.VMEM((2, 512, 256), F32),
+            pltpu.SemaphoreType.DMA((2,)),
+            *[pltpu.SemaphoreType.DMA((slots,))] * 2,
         ],
         compiler_params=pltpu.CompilerParams(
-            collective_id=0, has_side_effects=True, vmem_limit_bytes=48 * 2**20
+            collective_id=0, has_side_effects=True, vmem_limit_bytes=50 * 2**20
         ),
         name="power",
     )(samples, sketch)

time: 146 us -> 135 us (0.925)
  Pallas kernels: 144 us -> 134 us
    pallas_call x1, Pallas kernels: 138 us -> 128 us  [power(): pl.pallas_call(power_kernel, out_shape=(jax.ShapeDtypeStruct((8, 4, 16, 5...]
where the time goes in v4:
time: 135 us
  Pallas kernels  134 us (99%)
    pallas_call x1, Pallas kernels, power(): pl.pallas_call(power_kernel, out_shape=(jax.ShapeDtypeStruct((8, 4, 16, 5...  128 us
    pallas_call x1, Pallas kernels, finish(): pl.pallas_call(functools.partial(finish_kernel, scale), out_shape=(jax.Sh...  5.99 us

profile of v4, /device:TPU:1, one launch (start us, length us, event | category | flops | bytes accessed | tf_op | source)
XLA Modules:
  0.0 135.0 jit_solution(5439558010025649378)
XLA Ops:
  0.6 128.4 %power.1 = (f32[8,4,16,512]{3,2,1,0:T(8,128)S(1)}, f32[2,2,2,4,4,8,256]{6,5,4,3,2,1,0:T(8,128)S(1)}, f32[512,512]{1,0:T(8,128)S(1)}) custom-call(f32[2,512,512]{2,1,0:T(8,128)} %a_hbm.1, f32[2,512,256]{2,1,0:T(8,128)} %s_hbm.1), custom_call_target="tpu_custom_call" | custom-call | tf_op jit(solution)/shard_map/power/pallas_call | solution.py:591
  129.0 6.0 %finish.1 = (f32[2,512,512]{2,1,0:T(8,128)}, f32[2,512,512]{2,1,0:T(8,128)}) custom-call(f32[512,512]{1,0:T(8,128)S(1)} %bitcast.2, f32[2,512,256]{2,1,0:T(8,128)S(1)} %bitcast.3, f32[512,512]{1,0:T(8,128)S(1)} %get-tuple-element.7.m_ref), custom_call_target="tpu_custom_call" | custom-call | tf_op jit(solution)/shard_map/finish/pallas_call | solution.py:428

commit v5 on v4

--- a/solution.py
+++ b/solution.py
@@ -127,27 +127,24 @@
                 if step < 2:
                     self.push(way, quarter, 2 - step)
             yield
+        z = self.place.z
         for way, quarter in self.LEADS:
             self.pull(way, quarter, 1)
-        yield
+            self.full[z, quarter] = self.part[z, quarter]
+            for to in (1, -1):
+                self.push_on(to, quarter, 0)
+        yield
+
+    def gather_slot(self, way, quarter, dist):
+        return self.base + 28 + (0 if way > 0 else 14) + (quarter * 3 + dist if dist < 3 else 12 + quarter % 2)
+
+    def push_on(self, way, quarter, dist):
+        ref = self.full.at[wrap8(self.place.z - way * dist), quarter]
+        self.copies.send(self.gather_slot(way, quarter, dist), ref, ref, self.place.along_z(way))
 
     def gather_steps(self):
-        place, copies, full = self.place, self.copies, self.full
-        full[place.z] = self.part[place.z]
-        base = self.base + 28
-
-        def slot(way, quarter, dist):
-            return base + (0 if way > 0 else 14) + (quarter * 3 + dist if dist < 3 else 12 + quarter % 2)
-
-        def push(way, quarter, dist):
-            chunk = wrap8(place.z - way * dist)
-            ref = full.at[chunk, quarter]
-            copies.send(slot(way, quarter, dist), ref, ref, place.along_z(way))
-
+        copies, slot, push = self.copies, self.gather_slot, self.push_on
         order = self.LEADS + self.OTHERS
-        for way, quarter in order:
-            push(way, quarter, 0)
-        yield
         for dist in (1, 2):
             for way, quarter in order:
                 copies.arrived(slot(way, quarter, dist - 1))
@@ -362,9 +359,17 @@
         for m in range(7, 0, -1):
             q = q - jnp.where(sub < m, c[m] * inverse, 0.0) * row(q, m)
         rows = [row(q, k) for k in range(8)]
-        for v in range(g + 1, 16):
+        near = min(g + 3, 16)
+        if near < 16:
+            below = jnp.concatenate(groups[near:], 0)
+            zeros = [jnp.zeros((at, 128), F32)] if g else []
+            step = jnp.concatenate(zeros + [q, jnp.zeros((120 - at, 128), F32)], 0)
+            change = jnp.dot(below, step, precision=HI, preferred_element_type=F32)
+        for v in range(g + 1, near):
             cols = [col(groups[v], at + k) for k in range(8)]
             groups[v] = jnp.where(inside, 0.0, groups[v]) - dots(cols, rows)
+        for v in range(near, 16):
+            groups[v] = jnp.where(inside, 0.0, groups[v]) - change[8 * (v - near):8 * (v - near) + 8]
 
 
 def factor(m_ref, hook):
@@ -438,7 +443,8 @@
         name="finish",
     )(y, b, inverse)
 
-HOOKS = (0, 8, 16, 24, 32, 42, 50)
+ORDER = "ggygygygybgtgg"
+HOOKS = (3, 14, 25, 38, 48)
 
 
 def power_kernel(a_hbm, s_hbm, y_ref, b_ref, m_ref, x_hi, x_lo, xt_hi, xt_lo, t_hi, t_lo,
@@ -537,7 +543,6 @@
     run(steps)
     mine = z_part2[place.z].reshape(64, 512)
     steps = ring.gather_steps()
-    next(steps)
     real, imag = mine[:, :256], mine[:, 256:]
     tall = jnp.concatenate([real, imag], 0).T
     gram_r = jnp.dot(tall, jnp.concatenate([real, imag], 0), precision=HI, preferred_element_type=F32)
@@ -545,35 +550,32 @@
     low = lax.broadcasted_iota(jnp.int32, (256, 256), 0) >= lax.broadcasted_iota(jnp.int32, (256, 256), 1)
     g_part[...] = jnp.where(low, gram_r, gram_i).reshape(2, 4, 4, 8, 256)
     gram_steps = SumAll(place, copies, 2 * Z_SLOTS + ROW_SLOTS, g_part, g_core, g_line, g_point, g_z, g_ref).steps()
-    for _ in range(4):
-        next(gram_steps)
-    next(steps)
-    next(gram_steps)
-    next(steps)
-    next(gram_steps)
-    next(steps)
-    run(gram_steps)
-
-    def behind():
-        run(steps)
+    tail = SumRows(place, copies, 2 * Z_SLOTS + ROW_SLOTS + GRAM_SLOTS, r_part2, r_core2, r_line2,
+                   r_point2, b_ref).steps()
+
+    def start_b():
         chunks_to_t(y_ref)
         multiply(xt_hi, xt_lo, t_hi, t_lo, store_rows(r_part2), 1 - place.core)
-        tail = SumRows(place, copies, 2 * Z_SLOTS + ROW_SLOTS + GRAM_SLOTS, r_part2, r_core2, r_line2,
-                       r_point2, b_ref).steps()
         next(tail)
         multiply(xt_hi, xt_lo, t_hi, t_lo, store_rows(r_part2), place.core)
-        yield
-        yield from tail
-
-    rest = behind()
+
+    for turn in ORDER:
+        if turn == "g":
+            next(gram_steps)
+        elif turn == "y":
+            next(steps)
+        elif turn == "b":
+            start_b()
+        else:
+            next(tail)
 
     def hook(done):
         if done in HOOKS:
-            next(rest)
+            next(tail)
 
     set_gram(g_ref[...].reshape(256, 256), m_ref)
     factor(m_ref, hook)
-    run(rest)
+    run(tail)
     copies.finish()
 
 

time: 135 us -> 127 us (0.941)
  Pallas kernels: 134 us -> 126 us
    pallas_call x1, Pallas kernels: 128 us -> 120 us  [power(): pl.pallas_call(power_kernel, out_shape=(jax.ShapeDtypeStruct((8, 4, 16, 5...]
where the time goes in v5:
time: 127 us; the launch traced here: 126 us
  Pallas kernels  126 us (99%)
    pallas_call x1, Pallas kernels, power(): pl.pallas_call(power_kernel, out_shape=(jax.ShapeDtypeStruct((8, 4, 16, 5...  120 us
    pallas_call x1, Pallas kernels, finish(): pl.pallas_call(functools.partial(finish_kernel, scale), out_shape=(jax.Sh...  5.99 us

profile of v5, /device:TPU:1, one launch (start us, length us, event | category | flops | bytes accessed | tf_op | source)
XLA Modules:
  0.0 126.5 jit_solution(17301606983637964355)
XLA Ops:
  0.6 119.9 %power.1 = (f32[8,4,16,512]{3,2,1,0:T(8,128)S(1)}, f32[2,2,2,4,4,8,256]{6,5,4,3,2,1,0:T(8,128)S(1)}, f32[512,512]{1,0:T(8,128)S(1)}) custom-call(f32[2,512,512]{2,1,0:T(8,128)} %a_hbm.1, f32[2,512,256]{2,1,0:T(8,128)} %s_hbm.1), custom_call_target="tpu_custom_call" | custom-call | tf_op jit(solution)/shard_map/power/pallas_call | solution.py:593
  120.5 6.0 %finish.1 = (f32[2,512,512]{2,1,0:T(8,128)}, f32[2,512,512]{2,1,0:T(8,128)}) custom-call(f32[512,512]{1,0:T(8,128)S(1)} %bitcast.2, f32[2,512,256]{2,1,0:T(8,128)S(1)} %bitcast.3, f32[512,512]{1,0:T(8,128)S(1)} %get-tuple-element.7.m_ref), custom_call_target="tpu_custom_call" | custom-call | tf_op jit(solution)/shard_map/finish/pallas_call | solution.py:433

commit v6 on v5

--- a/solution.py
+++ b/solution.py
@@ -142,22 +142,28 @@
         ref = self.full.at[wrap8(self.place.z - way * dist), quarter]
         self.copies.send(self.gather_slot(way, quarter, dist), ref, ref, self.place.along_z(way))
 
-    def gather_steps(self):
-        copies, slot, push = self.copies, self.gather_slot, self.push_on
+    def gather_steps(self, use):
+        copies, slot, push, z = self.copies, self.gather_slot, self.push_on, self.place.z
+        use(z)
         order = self.LEADS + self.OTHERS
         for dist in (1, 2):
             for way, quarter in order:
                 copies.arrived(slot(way, quarter, dist - 1))
                 push(way, quarter, dist)
+            for way in (1, -1):
+                use(wrap8(z + way * dist))
             yield
         for way, quarter in self.LEADS:
             copies.arrived(slot(way, quarter, 2))
             push(way, quarter, 3)
         for way, quarter in self.OTHERS:
             copies.arrived(slot(way, quarter, 2))
+        for way in (1, -1):
+            use(wrap8(z + way * 3))
         yield
         for way, quarter in self.LEADS:
             copies.arrived(slot(way, quarter, 3))
+        use(wrap8(z + 4))
         yield
 
 
@@ -172,7 +178,7 @@
     def slot(self, h, s, kind, d):
         return self.base + 17 * (2 * h + s) + kind + d
 
-    def steps(self):
+    def steps(self, use=None):
         place, copies, slot = self.place, self.copies, self.slot
         part, full, core = self.part, self.full, place.core
         first = [place.at(0), place.at(1)]
@@ -224,10 +230,14 @@
                 copies.arrived(slot(h, s, LINE_BACK, d))
                 ref = full.at[h, core, s, lax.rem(first[h] - d + 4, 4)]
                 copies.send(slot(h, s, BACK, d), ref, ref, place.sibling())
+        if use:
+            use(core)
         yield
         for h, s in self.STREAMS:
             for d in range(4):
                 copies.arrived(slot(h, s, BACK, d))
+        if use:
+            use(1 - core)
         yield
 
 
@@ -402,7 +412,7 @@
     m_ref[:256, 256:] = -gram_i
 
 
-def finish_kernel(scale, y_ref, b_ref, m_ref, basis_ref, proj_ref, l_hi, l_lo):
+def finish_kernel(scale, y_ref, b_ref, m_ref, basis_ref, proj_ref, l_hi, l_lo, basis, proj, sems):
     for i in range(4):
         rows = slice(128 * i, 128 * i + 128)
         l_hi[rows, :], l_lo[rows, :] = split(m_ref[rows, :])
@@ -412,20 +422,28 @@
             lax.dot_general, dimension_numbers=(((1,), (1,)), ((), ())), preferred_element_type=F32)
         return dot(left_hi, right_hi) + (dot(left_hi, right_lo) + dot(left_lo, right_hi))
 
-    @pl.loop(0, 2)
-    def _(i):
+    copies = []
+
+    def out(ref, tile, p, rows, value):
+        tile[p, rows, :] = value
+        copy = pltpu.make_async_copy(tile.at[p, rows], ref.at[p, rows], sems.at[len(copies)])
+        copy.start()
+        copies.append(copy)
+
+    for i in range(2):
         rows = pl.ds(i * 256, 256)
         real, imag = y_ref[rows, :256], y_ref[rows, 256:]
-        basis_ref[0, rows, :] = product(*split(jnp.concatenate([real, -imag], 1)), l_hi[...], l_lo[...]) * scale
-        basis_ref[1, rows, :] = product(*split(jnp.concatenate([imag, real], 1)), l_hi[...], l_lo[...]) * scale
-
-    @pl.loop(0, 2)
-    def _(i):
-        rows = pl.ds(i * 256, 256)
-        real, imag = b_ref[0], b_ref[1]
-        hi, lo = l_hi[rows, :], l_lo[rows, :]
-        proj_ref[0, rows, :] = product(hi, lo, *split(jnp.concatenate([real, -imag], 1)))
-        proj_ref[1, rows, :] = product(hi, lo, *split(jnp.concatenate([imag, real], 1)))
+        for p, pair in enumerate(((real, -imag), (imag, real))):
+            value = product(*split(jnp.concatenate(pair, 1)), l_hi[...], l_lo[...]) * scale
+            out(basis_ref, basis, p, rows, value)
+    real, imag = b_ref[0], b_ref[1]
+    for p, pair in enumerate(((real, -imag), (imag, real))):
+        hi, lo = split(jnp.concatenate(pair, 1))
+        for i in range(2):
+            rows = pl.ds(i * 256, 256)
+            out(proj_ref, proj, p, rows, product(l_hi[rows, :], l_lo[rows, :], hi, lo))
+    for copy in copies:
+        copy.wait()
 
 
 def finish(y, b, inverse, scale):
@@ -434,10 +452,11 @@
         functools.partial(finish_kernel, scale),
         out_shape=(jax.ShapeDtypeStruct((2, 512, 512), F32),) * 2,
         in_specs=[vmem] * 3,
-        out_specs=(vmem,) * 2,
+        out_specs=(pl.BlockSpec(memory_space=pl.ANY),) * 2,
         scratch_shapes=[
-            pltpu.VMEM((512, 512), BF16),
-            pltpu.VMEM((512, 512), BF16),
+            *[pltpu.VMEM((512, 512), BF16)] * 2,
+            *[pltpu.VMEM((2, 512, 512), F32)] * 2,
+            pltpu.SemaphoreType.DMA((8,)),
         ],
         compiler_params=pltpu.CompilerParams(vmem_limit_bytes=48 * 2**20),
         name="finish",
@@ -513,27 +532,27 @@
             xt_hi[rows, lanes], xt_lo[rows, lanes] = split(block)
 
     run(steps)
-    run(ring.gather_steps())
-
-    def chunks_to_t(ref):
-        @pl.loop(0, 8)
+
+    def chunk_to_t(ref):
+        def use(chunk):
+            value = ref[chunk].reshape(64, 512)
+            set_pair(pl.multiple_of(chunk * 64, 64), value[:, :256], value[:, 256:], 1.0)
+        return use
+
+    run(ring.gather_steps(chunk_to_t(z_full)))
+    multiply(xt_hi, xt_lo, t_hi, t_lo, store_rows(r_part), 1 - place.core)
+
+    def rows_to_t(k):
+        @pl.loop(0, 4)
         def _(i):
-            value = ref[i].reshape(64, 512)
-            set_pair(i * 64, value[:, :256], value[:, 256:], 1.0)
-
-    chunks_to_t(z_full)
-    multiply(xt_hi, xt_lo, t_hi, t_lo, store_rows(r_part), 1 - place.core)
-    steps = SumRows(place, copies, Z_SLOTS, r_part, r_core, r_line, r_point, r_full).steps()
+            s, lines = i // 2, pl.ds(lax.rem(i, 2) * 2, 2)
+            set_pair(pl.multiple_of(k * 256 + i * 64, 64), r_full[0, k, s, lines].reshape(64, 256),
+                     r_full[1, k, s, lines].reshape(64, 256), -1.0)
+
+    steps = SumRows(place, copies, Z_SLOTS, r_part, r_core, r_line, r_point, r_full).steps(rows_to_t)
     next(steps)
     multiply(xt_hi, xt_lo, t_hi, t_lo, store_rows(r_part), place.core)
     run(steps)
-
-    for k in (0, 1):
-        for s in (0, 1):
-            @pl.loop(0, 2)
-            def _(i):
-                at, lines = k * 256 + s * 128 + i * 64, pl.ds(i * 2, 2)
-                set_pair(at, r_full[0, k, s, lines].reshape(64, 256), r_full[1, k, s, lines].reshape(64, 256), -1.0)
 
     ring = RingZ(place, copies, Z_SLOTS + ROW_SLOTS, z_part2, z_slots2, y_ref)
     steps = ring.scatter_steps()
@@ -542,7 +561,7 @@
     multiply(x_hi, x_lo, t_hi, t_lo, store_chunks(z_part2), 1 - far)
     run(steps)
     mine = z_part2[place.z].reshape(64, 512)
-    steps = ring.gather_steps()
+    steps = ring.gather_steps(chunk_to_t(y_ref))
     real, imag = mine[:, :256], mine[:, 256:]
     tall = jnp.concatenate([real, imag], 0).T
     gram_r = jnp.dot(tall, jnp.concatenate([real, imag], 0), precision=HI, preferred_element_type=F32)
@@ -554,7 +573,6 @@
                    r_point2, b_ref).steps()
 
     def start_b():
-        chunks_to_t(y_ref)
         multiply(xt_hi, xt_lo, t_hi, t_lo, store_rows(r_part2), 1 - place.core)
         next(tail)
         multiply(xt_hi, xt_lo, t_hi, t_lo, store_rows(r_part2), place.core)

time: 127 us -> 125 us (0.984)
  Pallas kernels: 126 us -> 124 us
    pallas_call x1, Pallas kernels: 5.99 us -> 4.33 us  [finish(): pl.pallas_call(functools.partial(finish_kernel, scale), out_shape=(jax.Sh...]
where the time goes in v6:
time: 125 us
  Pallas kernels  124 us (99%)
    pallas_call x1, Pallas kernels, power(): pl.pallas_call(power_kernel, out_shape=(jax.ShapeDtypeStruct((8, 4, 16, 5...  120 us
    pallas_call x1, Pallas kernels, finish(): pl.pallas_call(functools.partial(finish_kernel, scale), out_shape=(jax.Sh...  4.33 us

profile of v6, /device:TPU:1, one launch (start us, length us, event | category | flops | bytes accessed | tf_op | source)
XLA Modules:
  0.0 125.1 jit_solution(10922951646447429685)
XLA Ops:
  0.6 119.9 %power.1 = (f32[8,4,16,512]{3,2,1,0:T(8,128)S(1)}, f32[2,2,2,4,4,8,256]{6,5,4,3,2,1,0:T(8,128)S(1)}, f32[512,512]{1,0:T(8,128)S(1)}) custom-call(f32[2,512,512]{2,1,0:T(8,128)} %a_hbm.1, f32[2,512,256]{2,1,0:T(8,128)} %s_hbm.1), custom_call_target="tpu_custom_call" | custom-call | tf_op jit(solution)/shard_map/power/pallas_call | solution.py:611
  120.6 4.3 %finish.1 = (f32[2,512,512]{2,1,0:T(8,128)}, f32[2,512,512]{2,1,0:T(8,128)}) custom-call(f32[512,512]{1,0:T(8,128)S(1)} %bitcast.2, f32[2,512,256]{2,1,0:T(8,128)S(1)} %bitcast.3, f32[512,512]{1,0:T(8,128)S(1)} %get-tuple-element.7.m_ref), custom_call_target="tpu_custom_call" | custom-call | tf_op jit(solution)/shard_map/finish/pallas_call | solution.py:451

commit v7 on v6

--- a/solution.py
+++ b/solution.py
@@ -483,9 +483,15 @@
         ):
             t_hi[at, lanes], t_lo[at, lanes] = split(value)
 
+    far = 1 - place.z // 4
+
+    def tile_rows(i):
+        return pl.ds(pl.multiple_of(i * 256, 256), 256)
+
     fetches = [
-        pltpu.make_async_copy(src, dst, in_sem.at[n])
-        for n, (src, dst) in enumerate(((s_hbm, s_ref), (a_hbm, a_ref)))
+        pltpu.make_async_copy(s_hbm, s_ref, in_sem.at[0]),
+        pltpu.make_async_copy(a_hbm.at[:, tile_rows(far)], a_ref.at[:, tile_rows(far)], in_sem.at[1]),
+        pltpu.make_async_copy(a_hbm.at[:, tile_rows(1 - far)], a_ref.at[:, tile_rows(1 - far)], in_sem.at[2]),
     ]
     for fetch in fetches:
         fetch.start()
@@ -496,13 +502,15 @@
         rows = pl.ds(i * 64, 64)
         set_pair(i * 64, s_ref[0, rows, :], s_ref[1, rows, :], -1.0)
 
+    def split_tile(tile):
+        @pl.loop(0, 4)
+        def _(i):
+            rows = pl.ds(pl.multiple_of(tile * 256 + i * 64, 64), 64)
+            for p in (0, 1):
+                x_hi[rows, p * 512:(p + 1) * 512], x_lo[rows, p * 512:(p + 1) * 512] = split(a_ref[p, rows, :])
+
     fetches[1].wait()
-
-    @pl.loop(0, 8)
-    def _(i):
-        rows = pl.ds(i * 64, 64)
-        for p in (0, 1):
-            x_hi[rows, p * 512:(p + 1) * 512], x_lo[rows, p * 512:(p + 1) * 512] = split(a_ref[p, rows, :])
+    split_tile(far)
 
     def store_chunks(ref):
         def store(i, j, tile):
@@ -514,12 +522,13 @@
             ref[j, i] = tile.reshape(2, 4, 4, 8, 256)
         return store
 
-    far = 1 - place.z // 4
     ring = RingZ(place, copies, 0, z_part, z_slots, z_full)
     steps = ring.scatter_steps()
     multiply(x_hi, x_lo, t_hi, t_lo, store_chunks(z_part), far)
     all_here()
     next(steps)
+    fetches[2].wait()
+    split_tile(1 - far)
     multiply(x_hi, x_lo, t_hi, t_lo, store_chunks(z_part), 1 - far)
     next(steps)
 
@@ -629,7 +638,7 @@
             pltpu.VMEM((8, 8, 256), F32),
             pltpu.VMEM((2, 512, 512), F32),
             pltpu.VMEM((2, 512, 256), F32),
-            pltpu.SemaphoreType.DMA((2,)),
+            pltpu.SemaphoreType.DMA((3,)),
             *[pltpu.SemaphoreType.DMA((slots,))] * 2,
         ],
         compiler_params=pltpu.CompilerParams(

time: 125 us -> 125 us (level)
  no operation moved by 1% of the time
where the time goes in v7:
time: 125 us
  Pallas kernels  124 us (99%)
    pallas_call x1, Pallas kernels, power(): pl.pallas_call(power_kernel, out_shape=(jax.ShapeDtypeStruct((8, 4, 16, 5...  120 us
    pallas_call x1, Pallas kernels, finish(): pl.pallas_call(functools.partial(finish_kernel, scale), out_shape=(jax.Sh...  4.34 us

profile of v7, /device:TPU:1, one launch (start us, length us, event | category | flops | bytes accessed | tf_op | source)
XLA Modules:
  0.0 125.1 jit_solution(14736798079767859112)
XLA Ops:
  0.6 119.9 %power.1 = (f32[8,4,16,512]{3,2,1,0:T(8,128)S(1)}, f32[2,2,2,4,4,8,256]{6,5,4,3,2,1,0:T(8,128)S(1)}, f32[512,512]{1,0:T(8,128)S(1)}) custom-call(f32[2,512,512]{2,1,0:T(8,128)} %a_hbm.1, f32[2,512,256]{2,1,0:T(8,128)} %s_hbm.1), custom_call_target="tpu_custom_call" | custom-call | tf_op jit(solution)/shard_map/power/pallas_call | solution.py:620
  120.6 4.3 %finish.1 = (f32[2,512,512]{2,1,0:T(8,128)}, f32[2,512,512]{2,1,0:T(8,128)}) custom-call(f32[512,512]{1,0:T(8,128)S(1)} %bitcast.2, f32[2,512,256]{2,1,0:T(8,128)S(1)} %bitcast.3, f32[512,512]{1,0:T(8,128)S(1)} %get-tuple-element.7.m_ref), custom_call_target="tpu_custom_call" | custom-call | tf_op jit(solution)/shard_map/finish/pallas_call | solution.py:451
